TPU v7x, 32 devices: a whole 2x2x4 slice. The times are simulated.
32 devices in a mesh: ex: 8 (over y, x, core), feat: 4 (over z).
Axes of the slice: x: 2, y: 2, z: 4, core: 2. Of those that a mesh axis runs over, the one named last changes fastest.
Arguments:
- features: bfloat16 [16384, 2048], P('ex', 'feat'), may hold values from -0.125 to 0.125
- weights: float32 [2048], P('feat'), may hold values from -6 to 6
- labels: int32 [16384], P('ex'), may hold values 0 or 1
- signs: int32 [16384], P('ex'), may hold values from -1 to 1, as said below
- samples: int32 [2048], replicated, may hold values from 0 to 16383
- radius: float32 [1], replicated, may hold values from 0.1 to 0.25
Outputs:
- new_weights: float32 [2048], P('feat')
Inputs may be any that keep to these rules, and one draw needn't show every extreme that they name: `signs`: each entry is -1 or +1.
All inputs are finite; a program needn't handle non-finite values. No bound on the sum of `labels` on one device may be relied on, other than what follows from the above.
Results may differ from a plain program's by a relative error of at most 0.00067.
Values may be sent and summed in bfloat16 or wider, within the bound.
No kernel may reach another device: no remote copies, remote signals or barrier semaphores. Data moves between devices by JAX's collectives and lax.ppermute only.
A program may use at most 192 MiB of HBM per device.

v0:
```python
import math

import jax
import jax.numpy as jnp
from jax import lax
from jax.sharding import PartitionSpec as P

D = 2048
ITERS = 4


REG = 0.02


def from_partner(value, axis, bit):
    mask = 2**bit
    pairs = [(source, source ^ mask) for source in range(lax.axis_size(axis))]
    return lax.ppermute(value, axis, pairs)


def parity_bits(common, bit_total):
    parity = jnp.zeros(common.shape, jnp.int32)
    for bit_number in range(bit_total):
        parity = parity ^ common >> bit_number & 1
    return parity


def sign_table(length):
    indices = lax.iota(jnp.int32, length)
    parity = parity_bits(indices[:, None] & indices[None, :], max(1, length.bit_length()))
    return 1 - 2 * parity


def local_mix(signed):
    row_count, feat_width = signed.shape
    levels = row_count.bit_length() - 1
    outer = 2 ** (levels // 2)
    inner = row_count // outer
    shaped = signed.reshape(outer, inner, feat_width)
    first = jnp.einsum(
        "jk,ikd->ijd",
        sign_table(inner).astype(jnp.bfloat16),
        shaped,
        preferred_element_type=jnp.float32,
    )
    second = jnp.einsum(
        "hi,ijd->hjd", sign_table(outer).astype(jnp.float32), first, precision=lax.Precision.HIGHEST
    )
    return second.reshape(row_count, feat_width)


def precondition(factor_lower, residual):
    middle = lax.linalg.triangular_solve(
        factor_lower, residual[:, None], left_side=True, lower=True
    )
    return lax.linalg.triangular_solve(
        factor_lower, middle, left_side=True, lower=True, transpose_a=True
    )[:, 0]


def local(features, weights, labels, signs, samples, radius):
    highest = lax.Precision.HIGHEST
    row_count, feat_width = features.shape
    ex_count = lax.axis_size("ex")
    ex_index = lax.axis_index("ex")
    feat_index = lax.axis_index("feat")
    total_rows = row_count * ex_count
    sample_count = samples.shape[0]
    ridge = REG / D
    dense = features.astype(jnp.float32)
    margins = lax.psum(jnp.dot(dense, weights, precision=highest), "feat")
    probability = 1.0 / (1.0 + jnp.exp(-margins))
    curvature = probability * (1.0 - probability)
    grad_part = jnp.dot(probability - labels.astype(jnp.float32), dense, precision=highest)
    gradient = lax.psum(grad_part, "ex") / total_rows + ridge * weights
    weighted = (jnp.sqrt(curvature)[:, None] * dense).astype(jnp.bfloat16)
    weighted_float = weighted.astype(jnp.float32)
    signed = weighted * signs.astype(jnp.bfloat16)[:, None]
    mixed = local_mix(signed)
    for bit_index in range(ex_count.bit_length() - 1):
        partner = from_partner(mixed, "ex", bit_index)
        upper = ex_index >> bit_index & 1
        mixed = jnp.where(upper == 0, mixed + partner, partner - mixed)
    local_place = samples - ex_index * row_count
    owned = ((local_place >= 0) & (local_place < row_count)).astype(jnp.float32)
    picked = mixed[jnp.clip(local_place, 0, row_count - 1)] * owned[:, None]
    summed = lax.psum_scatter(picked, "ex", scatter_dimension=0, tiled=True)
    sketch = (summed * (1.0 / math.sqrt(total_rows * sample_count))).astype(jnp.bfloat16)
    wide_sketch = lax.all_gather(sketch, "feat", axis=1, tiled=True)
    piece = lax.all_gather(wide_sketch, "ex", axis=0, tiled=True)
    gram = lax.dot_general(
        piece, piece, (((0,), (0,)), ((), ())), preferred_element_type=jnp.float32
    )
    gram = gram + ridge * jnp.eye(D, dtype=jnp.float32)
    factor_lower = jnp.linalg.cholesky(gram)

    def apply_inverse(residual_part):
        gathered = lax.all_gather(residual_part, "feat", axis=0, tiled=True)
        return (gathered, precondition(factor_lower, gathered))

    solution = jnp.zeros((feat_width,), jnp.float32)
    residual = -gradient
    gathered, solved = apply_inverse(residual)
    inner_now = jnp.dot(gathered, solved)
    direction = solved
    for number in range(ITERS):
        dir_part = lax.dynamic_slice_in_dim(direction, feat_index * feat_width, feat_width, 0)
        row_part = jnp.dot(weighted_float, dir_part, precision=highest)
        row_sums = lax.psum(row_part, "feat")
        column_part = jnp.dot(row_sums, weighted_float, precision=highest)
        curved = lax.psum(column_part, "ex") / total_rows + ridge * dir_part
        curvature_sum = lax.psum(jnp.dot(dir_part, curved), "feat")
        step_size = inner_now / curvature_sum
        solution = solution + step_size * dir_part
        residual = residual - step_size * curved
        if number + 1 < ITERS:
            gathered, solved = apply_inverse(residual)
            inner_next = jnp.dot(gathered, solved)
            direction = solved + inner_next / inner_now * direction
            inner_now = inner_next
    length_sq = lax.psum(jnp.dot(solution, solution), "feat")
    scale_step = jnp.minimum(1.0, radius[0] * math.sqrt(D) / jnp.sqrt(length_sq + 1e-06))
    return weights + scale_step * solution


def solution(mesh):
    in_specs = (P("ex", "feat"), P("feat"), P("ex"), P("ex"), P(), P())
    out_specs = P("feat")
    return jax.shard_map(local, mesh=mesh, in_specs=in_specs, out_specs=out_specs, check_vma=False)
```

profile of v0, /device:TPU:0, one launch (start us, length us, event | category | flops | bytes accessed | tf_op | source)
XLA Modules:
  0.0 1574.5 jit_solution(6588746208548607100)
XLA Ops:
  9.8 13.7 psum.105
  38.1 7.5 collective-permute-done
  53.5 91.4 %collective-permute-done.1 = f32[2048,512]{1,0:T(8,128)} collective-permute-done((f32[2048,512]{1,0:T(8,128)}, f32[2048,512]{1,0:T(8,128)}, u32[]{:S(2)}, u32[]{:S(2)}) %collective-permute-start.1) | collective-permute-done | bytes 4194336 | tf_op jit(solution)/shard_map/ppermute | solution.py:18
  153.0 90.6 %collective-permute-done.2 = f32[2048,512]{1,0:T(8,128)} collective-permute-done((f32[2048,512]{1,0:T(8,128)}, f32[2048,512]{1,0:T(8,128)}, u32[]{:S(2)}, u32[]{:S(2)}) %collective-permute-start.2) | collective-permute-done | bytes 4194336 | tf_op jit(solution)/shard_map/ppermute | solution.py:18
  250.1 11.7 gather_fusion
  266.5 49.7 %reduce-scatter.2.cloned.1.call-done = f32[256,512]{1,0:T(8,128)} async-done(((f32[2048,512]{1,0:T(8,128)}), f32[256,512]{1,0:T(8,128)}) %reduce-scatter.2.cloned.1.call-update) | async-done | bytes 524304 | tf_op jit(solution)/shard_map/reduce_scatter | solution.py:87
  318.0 28.0 %all-gather.7.cloned.1.call-done = bf16[256,2048]{1,0:T(8,128)(2,1)} async-done(((bf16[256,512]{1,0:T(8,128)(2,1)}), bf16[256,2048]{1,0:T(8,128)(2,1)}) %all-gather.7.cloned.1.call-update) | async-done | bytes 1048592 | tf_op jit(solution)/shard_map/all_gather | solution.py:89
  348.5 13.7 psum.106
  362.2 11.9 all-gather
  374.1 27.9 %all-gather.9.cloned.1.call-done = bf16[2048,2048]{1,0:T(8,128)(2,1)} async-done(((bf16[256,2048]{1,0:T(8,128)(2,1)}), bf16[2048,2048]{1,0:T(8,128)(2,1)}) %all-gather.9.cloned.1.call-update) | async-done | bytes 8388624 | tf_op jit(solution)/shard_map/all_gather | solution.py:90
  402.0 24.3 %fusion.556 = f32[2048,2048]{1,0:T(8,128)} fusion(bf16[2048,2048]{1,0:T(8,128)(2,1)} %all-gather.9.cloned.1.call-done), kind=kOutput, calls=%fused_computation.1866 | convolution fusion | flops 17179869184 | bytes 25165824 | tf_op jit(solution)/shard_map/dot_general | solution.py:91
  426.3 17.6 %copy.12 = f32[2048,2048]{0,1:T(8,128)} copy(f32[2048,2048]{1,0:T(8,128)} %fusion.556) | data formatting | bytes 33554432 | tf_op jit(solution)/shard_map/dot_general | solution.py:91
  443.9 12.5 fusion.1
  462.1 11.7 cholesky.456
  473.8 9.8 custom-call.129
  483.7 7.8 cholesky.486
  496.8 11.9 cholesky.479
  509.3 9.8 custom-call.130
  524.4 11.7 cholesky.502
  537.4 9.8 custom-call.131
  553.6 11.7 cholesky.523
  566.6 9.8 custom-call.132
  583.3 11.7 cholesky.960
  596.3 9.8 custom-call.133
  613.2 11.9 cholesky.980
  626.3 9.8 custom-call.134
  643.3 11.7 cholesky.1000
  656.3 10.0 custom-call.135
  673.8 11.7 cholesky.1020
  686.8 10.2 custom-call.136
  704.3 11.7 cholesky.1040
  717.3 9.8 custom-call.137
  734.5 11.7 cholesky.1060
  747.6 9.8 custom-call.138
  764.5 11.7 cholesky.1080
  777.5 9.8 custom-call.139
  793.7 12.1 cholesky.1100
  807.1 9.8 custom-call.140
  822.8 11.7 cholesky.1120
  835.9 9.9 custom-call.141
  851.1 11.7 cholesky.1140
  864.1 9.8 custom-call.142
  878.3 12.1 cholesky.1160
  891.6 9.8 custom-call.143
  904.9 11.7 cholesky.1178
  928.4 12.5 select_select_fusion
  940.9 56.5 %while.16 = (s32[]{:T(128)}, f32[2048,2048]{1,0:T(8,128)}, s32[16,2]{0,1:T(2,128)S(1)}, f32[16,128,128]{2,1,0:T(8,128)}, s32[]{:T(128)}) while((s32[]{:T(128)}, f32[2048,2048]{1,0:T(8,128)}, s32[16,2]{0,1:T(2,128)S(1)}, f32[16,128,128]{2,1,0:T(8,128)}, s32[]{:T(128)}) %tuple.563), condition=%wide.while_cond.1, body=%wide.while_body.1.sunk | while | flops 2 | bytes 132705 | solution.py:56
  997.4 158.1 %custom-call.151 = f32[16,128,128]{1,2,0:T(8,128)S(1)} custom-call(f32[16,128,128]{2,1,0:T(8,128)} %get-tuple-element.60), custom_call_target="InvertDiagBlocksLowerTriangular" | custom-call | tf_op jit(solution)/shard_map/triangular_solve/custom-call.32 | solution.py:56
  1210.8 11.8 psum.107
  1223.6 11.8 psum.108
  1236.0 9.0 psum.109
  1246.8 11.9 all-gather.1
  1315.6 9.6 psum.110
  1326.1 11.8 psum.111
  1338.6 9.9 psum.112
  1349.8 11.9 all-gather.2
  1418.6 8.6 psum.113
  1428.2 11.8 psum.114
  1441.3 10.8 psum.115
  1453.4 11.9 all-gather.3
  1522.4 8.5 psum.116
  1531.9 11.8 psum.117
  1544.3 11.0 psum.118
  1557.3 9.0 psum.119
  (889 shorter events, 452.4 us)
Async XLA Ops:
  6.5 309.6 %reduce-scatter.2.cloned.1.call-start = ((), (), s32[]{:S(2)}) async-start(), calls=%async_computation.1 | async-start | bytes 4718592 | tf_op jit(solution)/shard_map/reduce_scatter | solution.py:87
  33.7 119.2 %copy-start.1 = (s32[2048]{0:T(1024)S(1)}, s32[2048]{0:T(1024)}, u32[]{:S(2)}) copy-start(s32[2048]{0:T(1024)} %param.14) | copy-start | bytes 24580
  38.1 7.5 collective-permute-start
  52.0 92.9 %collective-permute-start.1 = (f32[2048,512]{1,0:T(8,128)}, f32[2048,512]{1,0:T(8,128)}, u32[]{:S(2)}, u32[]{:S(2)}) collective-permute-start(f32[2048,512]{1,0:T(8,128)} %subtract_select_fusion.2), channel_id=1, source_target_pairs={{0,8},{4,12},{8,0},{12,4},{16,24},{20,28},{24,16},{28,20},{1,9},{5... | collective-permute-start | bytes 12582920 | tf_op jit(solution)/shard_map/ppermute | solution.py:18
  151.4 92.1 %collective-permute-start.2 = (f32[2048,512]{1,0:T(8,128)}, f32[2048,512]{1,0:T(8,128)}, u32[]{:S(2)}, u32[]{:S(2)}) collective-permute-start(f32[2048,512]{1,0:T(8,128)} %subtract_select_fusion.1), channel_id=1, source_target_pairs={{0,16},{4,20},{8,24},{12,28},{16,0},{20,4},{24,8},{28,12},{1,17},{... | collective-permute-start | bytes 12582920 | tf_op jit(solution)/shard_map/ppermute | solution.py:18
  261.9 100.3 %copy-start.2 = (f32[512]{0:T(512)S(1)}, f32[512]{0:T(512)}, u32[]{:S(2)}) copy-start(f32[512]{0:T(512)} %param.11) | copy-start | bytes 6148
  266.4 79.6 %all-gather.7.cloned.1.call-start = ((), (), s32[]{:S(2)}) async-start(), calls=%async_computation.2 | async-start | bytes 1310720 | tf_op jit(solution)/shard_map/all_gather | solution.py:89
  317.9 84.1 %all-gather.9.cloned.1.call-start = ((), (), s32[]{:S(2)}) async-start(), calls=%async_computation.3 | async-start | bytes 9437184 | tf_op jit(solution)/shard_map/all_gather | solution.py:90
  456.4 5.7 copy-start
Sparse Core Ops, SparseCore 0:
  266.5 49.5 reduce-scatter.1
  318.1 27.9 all-gather.6
  348.1 53.9 all-gather.8
where the time goes:
time: 1590 us; the launch traced here: 1570 us
  other arithmetic  575 us (36%)
  matrix products  346 us (22%)
  waiting for transfers between devices  295 us (19%)
  blocking collectives  210 us (13%)
  local copies, waits for them, and re-layouts  109 us (7%)
  between operations  36.1 us (2%)
    another operation x62, other arithmetic, local(): factor_lower = jnp.linalg.cholesky(gram)  356 us
    ppermute x3, waiting for transfers between devices, from_partner(): return lax.ppermute(value, axis, pairs)  189 us
    another operation x4, other arithmetic, precondition(): lax.linalg.triangular_solve(factor_lower, middle, left_side=True, lower=T...  171 us
    another operation x124, matrix products, precondition(): lax.linalg.triangular_solve(factor_lower, residual[:, None], left_side=Tr...  107 us
    another operation x124, matrix products, precondition(): lax.linalg.triangular_solve(factor_lower, middle, left_side=True, lower=T...  99.3 us
    another operation x30, matrix products, local(): factor_lower = jnp.linalg.cholesky(gram)  92.4 us
    another operation x97, local copies, waits for them, and re-layouts, precondition(): lax.linalg.triangular_solve(factor_lower, middle, left_side=True, lower=T...  56.9 us
    reduce_scatter x1, waiting for transfers between devices, local(): summed = lax.psum_scatter(picked, 'ex', scatter_dimension=0, tiled=True)  49.7 us
  transfers between devices with their start and end apart: 6, of which 6 were waited for; matrix products, arithmetic and copies ran while one was open for 0% of the time, Pallas kernels for 0%

commit v1 on v0

v1 whole, which is shorter than its diff:
```python
import math

import jax
import jax.numpy as jnp
from jax import lax
from jax.experimental import pallas as pl
from jax.experimental.pallas import tpu as pltpu
from jax.sharding import PartitionSpec as P

D = 2048
ITERS = 4
REG = 0.02
BLOCK = 128
PIVOTS = 8
CHUNK = 256


def split(value):
    high = value.astype(jnp.bfloat16)
    low = (value - high.astype(jnp.float32)).astype(jnp.bfloat16)
    return high, low


def invert_block(block):
    tiles = BLOCK // PIVOTS
    lane = lax.broadcasted_iota(jnp.int32, (PIVOTS, BLOCK), 1)
    sub = lax.broadcasted_iota(jnp.int32, (PIVOTS, BLOCK), 0)
    unit = (lane == sub).astype(jnp.float32)
    inside = lane < PIVOTS

    def step(_, held):
        rows = held[0]
        cols = [jnp.broadcast_to(rows[:, j : j + 1], (PIVOTS, BLOCK)) for j in range(PIVOTS)]
        rows = jnp.where(inside, unit, rows)
        for j in range(PIVOTS):
            inverse = 1.0 / cols[j][j : j + 1, :]
            factor = cols[j] - (sub == j).astype(jnp.float32)
            for c in range(j + 1, PIVOTS):
                cols[c] = cols[c] - factor * (cols[c][j : j + 1, :] * inverse)
            rows = rows - factor * (rows[j : j + 1, :] * inverse)
        fresh = []
        for tile in held[1:]:
            total = jnp.where(inside, 0.0, tile)
            for j in range(PIVOTS):
                total = total - tile[:, j : j + 1] * rows[j : j + 1, :]
            fresh.append(total)
        fresh.append(rows)
        return tuple(pltpu.roll(tile, BLOCK - PIVOTS, 1) for tile in fresh)

    held = tuple(block[t * PIVOTS : (t + 1) * PIVOTS, :] for t in range(tiles))
    held = lax.fori_loop(0, tiles, step, held)
    return jnp.concatenate(held, axis=0)


def factor_kernel(gram_ref, out_ref, inv_ref, work, left, right, diag, sem):
    size = gram_ref.shape[0]
    blocks = size // BLOCK
    copy = pltpu.make_async_copy(gram_ref, work, sem)
    copy.start()
    copy.wait()
    eye = (
        lax.broadcasted_iota(jnp.int32, (BLOCK, BLOCK), 0)
        == lax.broadcasted_iota(jnp.int32, (BLOCK, BLOCK), 1)
    ).astype(jnp.float32)

    def outer(k, _):
        here = pl.ds(pl.multiple_of(k * BLOCK, BLOCK), BLOCK)
        inverse = invert_block(work[here, here])
        inv_ref[here, :] = inverse
        inv_high, inv_low = split(inverse)
        diag[0:BLOCK, :] = inv_high
        diag[BLOCK : 2 * BLOCK, :] = inv_high
        diag[2 * BLOCK : 3 * BLOCK, :] = inv_low
        diag[3 * BLOCK : 4 * BLOCK, :] = inv_low
        work[here, here] = eye
        for c in range(size // CHUNK):
            cols = slice(c * CHUNK, (c + 1) * CHUNK)
            high, low = split(work[here, cols])
            right[0:BLOCK, cols] = high
            right[BLOCK : 2 * BLOCK, cols] = high
            right[2 * BLOCK : 3 * BLOCK, cols] = low
            right[3 * BLOCK : 4 * BLOCK, cols] = low

        def update(m, _):
            rows = pl.ds(pl.multiple_of(m * CHUNK, CHUNK), CHUNK)
            panel = work[rows, here]
            high, low = split(panel)
            wide = jnp.concatenate([high, low, high, low], axis=1)
            scaled = jnp.dot(wide, diag[...], preferred_element_type=jnp.float32)
            place = m * CHUNK + lax.broadcasted_iota(jnp.int32, (CHUNK, BLOCK), 0)
            later = place >= (k + 1) * BLOCK
            scaled = jnp.where(later, scaled, 0.0)
            work[rows, here] = jnp.where(later, 0.0, panel)
            high, low = split(scaled)
            wide = jnp.concatenate([high, low, high, low], axis=1)
            for c in range(size // CHUNK):
                cols = slice(c * CHUNK, (c + 1) * CHUNK)
                work[rows, cols] = work[rows, cols] - jnp.dot(
                    wide, right[:, cols], preferred_element_type=jnp.float32
                )
            return 0

        lax.fori_loop((k + 1) * BLOCK // CHUNK, size // CHUNK, update, 0)
        return 0

    lax.fori_loop(0, blocks, outer, 0)

    def clear(k, _):
        here = pl.ds(pl.multiple_of(k * BLOCK, BLOCK), BLOCK)
        for c in range(blocks):
            cols = slice(c * BLOCK, (c + 1) * BLOCK)
            work[here, cols] = jnp.where(c > k, 0.0, work[here, cols])
        return 0

    lax.fori_loop(0, blocks, clear, 0)
    copy = pltpu.make_async_copy(work, out_ref, sem)
    copy.start()
    copy.wait()


def factor(gram, interpret=False):
    size = gram.shape[0]
    return pl.pallas_call(
        factor_kernel,
        in_specs=[pl.BlockSpec(memory_space=pl.ANY)],
        out_specs=[pl.BlockSpec(memory_space=pl.ANY), pl.BlockSpec(memory_space=pltpu.VMEM)],
        out_shape=[
            jax.ShapeDtypeStruct((size, size), jnp.float32),
            jax.ShapeDtypeStruct((size, BLOCK), jnp.float32),
        ],
        scratch_shapes=[
            pltpu.VMEM((size, size), jnp.float32),
            pltpu.VMEM((16, 128), jnp.float32),
            pltpu.VMEM((4 * BLOCK, size), jnp.bfloat16),
            pltpu.VMEM((4 * BLOCK, BLOCK), jnp.bfloat16),
            pltpu.SemaphoreType.DMA,
        ],
        compiler_params=pltpu.CompilerParams(vmem_limit_bytes=40 * 2**20),
        interpret=interpret,
    )(gram)


def local(features, weights, labels, signs, samples, radius):
    highest = lax.Precision.HIGHEST
    row_count, feat_width = features.shape
    ex_count = lax.axis_size("ex")
    feat_count = lax.axis_size("feat")
    ex_index = lax.axis_index("ex")
    feat_index = lax.axis_index("feat")
    total_rows = row_count * ex_count
    sample_count = samples.shape[0]
    ridge = REG / D
    dense = features.astype(jnp.float32)
    margins = lax.psum(jnp.dot(dense, weights, precision=highest), "feat")
    probability = 1.0 / (1.0 + jnp.exp(-margins))
    curvature = probability * (1.0 - probability)
    weighted = (jnp.sqrt(curvature)[:, None] * dense).astype(jnp.bfloat16)
    signed = weighted * signs.astype(jnp.bfloat16)[:, None]
    places = ex_index * row_count + lax.iota(jnp.int32, row_count)
    odd = lax.population_count(samples[:, None] & places[None, :]) & 1
    table = (1 - 2 * odd).astype(jnp.bfloat16)
    mixed = jnp.dot(table, signed, preferred_element_type=jnp.float32)
    summed = lax.psum_scatter(mixed, "ex", scatter_dimension=0, tiled=True)
    sketch = (summed * (1.0 / math.sqrt(total_rows * sample_count))).astype(jnp.bfloat16)
    wide_sketch = lax.all_gather(sketch, "feat", axis=1, tiled=True)
    piece = lax.all_gather(wide_sketch, "ex", axis=0, tiled=True)
    gram = lax.dot_general(
        piece, piece, (((0,), (0,)), ((), ())), preferred_element_type=jnp.float32
    )
    gram = gram + ridge * jnp.eye(D, dtype=jnp.float32)
    lower, inverses = factor(gram)
    inverses = inverses.reshape(D // BLOCK, BLOCK, BLOCK)

    def apply_inverse(residual):
        middle = jnp.dot(lower, residual, precision=highest).reshape(D // BLOCK, BLOCK)
        middle = jnp.einsum("kij,kj->ki", inverses, middle, precision=highest).reshape(D)
        return jnp.dot(middle, lower, precision=highest)

    def whole(part):
        wide = jnp.zeros((D,), jnp.float32)
        return lax.dynamic_update_slice_in_dim(wide, part, feat_index * feat_width, 0)

    grad_part = jnp.dot(probability - labels.astype(jnp.float32), dense, precision=highest)
    own_rows = lax.all_to_all(weighted, "feat", split_axis=0, concat_axis=1, tiled=True)
    own_rows = own_rows.astype(jnp.float32)
    own_weights = jnp.where(ex_index == 0, weights, 0.0)
    residual = -lax.psum(whole(grad_part / total_rows + ridge * own_weights), ("ex", "feat"))

    def curve(direction):
        rows = jnp.dot(own_rows, direction, precision=highest)
        return jnp.dot(rows, own_rows, precision=highest)

    solution = jnp.zeros((D,), jnp.float32)
    solved = apply_inverse(residual)
    inner_now = jnp.dot(residual, solved)
    direction = solved
    for number in range(ITERS):
        curved = lax.psum(curve(direction), ("ex", "feat")) / total_rows + ridge * direction
        step_size = inner_now / jnp.dot(direction, curved)
        solution = solution + step_size * direction
        if number + 1 < ITERS:
            residual = residual - step_size * curved
            solved = apply_inverse(residual)
            inner_next = jnp.dot(residual, solved)
            direction = solved + inner_next / inner_now * direction
            inner_now = inner_next
    length_sq = jnp.dot(solution, solution)
    scale_step = jnp.minimum(1.0, radius[0] * math.sqrt(D) / jnp.sqrt(length_sq + 1e-06))
    own = lax.dynamic_slice_in_dim(solution, feat_index * feat_width, feat_width, 0)
    return weights + scale_step * own


def solution(mesh):
    in_specs = (P("ex", "feat"), P("feat"), P("ex"), P("ex"), P(), P())
    out_specs = P("feat")
    return jax.shard_map(local, mesh=mesh, in_specs=in_specs, out_specs=out_specs, check_vma=False)
```

time: 1590 us -> 703 us (0.44)
  other arithmetic: 575 us -> 11 us
  waiting for transfers between devices: 295 us -> 77.8 us
  matrix products: 346 us -> 168 us
  Pallas kernels: 0 us -> 166 us
  local copies, waits for them, and re-layouts: 109 us -> 3.46 us
  blocking collectives: 210 us -> 242 us
    another operation x66 -> x0, other arithmetic: 527 us -> none  [the longest x62 356 us: local(): factor_lower = jnp.linalg.cholesky(gram)]
    another operation x278 -> x0, matrix products: 298 us -> none  [the longest x124 107 us: precondition(): lax.linalg.triangular_solve(factor_lower, residual[:, None], left_side=Tr...]
    ppermute x3 -> x0, waiting for transfers between devices: 189 us -> none  [from_partner(): return lax.ppermute(value, axis, pairs)]
    pallas_call x0 -> x1, Pallas kernels: none -> 166 us  [factor(): pl.pallas_call(factor_kernel, in_specs=[pl.BlockSpec(memory_space=pl.ANY)...]
    dot_general x10 -> x21, matrix products: 17.1 us -> 139 us  [the longest x4 71 us: apply_inverse(): jnp.dot(lower, residual, precision=highest).reshape(D // BLOCK, BLOCK)]
    psum x14 -> x5, blocking collectives: 149 us -> 228 us  [the longest x4 160 us: local(): lax.psum(curve(direction), ('ex', 'feat')) / total_rows + ridge * direction]
    another operation x113 -> x0, local copies, waits for them, and re-layouts: 64.8 us -> none  [the longest x97 56.9 us: precondition(): lax.linalg.triangular_solve(factor_lower, middle, left_side=True, lower=T...]
    all_gather x4 -> x0, blocking collectives: 47.5 us -> none  [apply_inverse(): gathered = lax.all_gather(residual_part, 'feat', axis=0, tiled=True)]
  transfers between devices with their start and end apart: 6 -> 4, of which waited for: 6 -> 2; matrix products, arithmetic and copies ran while one was open for 0% -> 1% of each run, Pallas kernels for 0% -> 0%
where the time goes in v1:
time: 703 us; the launch traced here: 696 us
  blocking collectives  242 us (34%)
  matrix products  168 us (24%)
  Pallas kernels  166 us (24%)
  waiting for transfers between devices  77.8 us (11%)
  between operations  23.7 us (3%)
  other arithmetic  11 us (2%)
    pallas_call x1, Pallas kernels, factor(): pl.pallas_call(factor_kernel, in_specs=[pl.BlockSpec(memory_space=pl.ANY)...  166 us
    psum x4, blocking collectives, local(): lax.psum(curve(direction), ('ex', 'feat')) / total_rows + ridge * direction  160 us
    dot_general x4, matrix products, apply_inverse(): jnp.dot(lower, residual, precision=highest).reshape(D // BLOCK, BLOCK)  71 us
    psum x1, blocking collectives, local(): lax.psum(whole(grad_part / total_rows + ridge * own_weights), ('ex', 'fea...  67.6 us
    reduce_scatter x1, waiting for transfers between devices, local(): summed = lax.psum_scatter(mixed, 'ex', scatter_dimension=0, tiled=True)  49.7 us
    dot_general x4, matrix products, apply_inverse(): return jnp.dot(middle, lower, precision=highest)  43 us
    all_gather x1, waiting for transfers between devices, local(): wide_sketch = lax.all_gather(sketch, 'feat', axis=1, tiled=True)  28 us
    dot_general x1, matrix products, local(): lax.dot_general(piece, piece, (((0,), (0,)), ((), ())), preferred_element...  24.9 us
  transfers between devices with their start and end apart: 4, of which 2 were waited for; matrix products, arithmetic and copies ran while one was open for 1% of the time, Pallas kernels for 0%

profile of v1, /device:TPU:0, one launch (start us, length us, event | category | flops | bytes accessed | tf_op | source)
XLA Modules:
  0.0 696.2 jit_solution(18357944600357751048)
XLA Ops:
  6.5 0.0 reduce-scatter.2.cloned.1.call-start
  6.5 3.3 fusion.11
  9.9 13.7 %psum.42 = f32[2048]{0:T(1024)S(1)} all-reduce(f32[2048]{0:T(1024)S(1)} %bitcast.178), channel_id=1, replica_groups=mesh['ex'=8,'feat'=4] {'feat'}, use_global_device_ids=true, to_apply=%region_0.0 | all-reduce | flops 2048 | bytes 16384 | tf_op jit(solution)/shard_map/psum | solution.py:154
  23.6 0.7 convert_subtract_fusion
  24.3 2.0 multiply_convert_fusion
  26.3 0.0 copy-start.2
  26.3 0.7 convert_element_type.24
  27.1 0.7 copy-done.2
  27.7 7.3 %fusion = f32[2048,512]{1,0:T(8,128)} fusion(s32[2048]{0:T(1024)S(1)} %iota_add_fusion, s32[2048]{0:T(1024)} %param.10, bf16[2048,512]{1,0:T(8,128)(2,1)S(1)} %multiply_convert_fusion, bf16[2048]{0:T(1024)(128)(2,1)S(1)} %convert_element_type.24), kind=kOutput, calls=%fused_computation.3 | convolution fusion | flops 4321181696 | bytes 6311936 | tf_op jit(solution)/shard_map/dot_general | solution.py:162
  35.0 0.0 copy-start.1
  35.0 0.0 reduce-scatter.2.cloned.1.call-update
  35.1 0.0 all-gather.3.cloned.1.call-start
  35.1 49.7 %reduce-scatter.2.cloned.1.call-done = f32[256,512]{1,0:T(8,128)} async-done(((f32[2048,512]{1,0:T(8,128)}), f32[256,512]{1,0:T(8,128)}) %reduce-scatter.2.cloned.1.call-update) | async-done | bytes 524304 | tf_op jit(solution)/shard_map/reduce_scatter | solution.py:163
  84.8 1.8 multiply_convert_fusion.1
  86.6 0.0 all-gather.3.cloned.1.call-update
  86.6 0.0 all-gather.5.cloned.1.call-start
  86.6 28.0 %all-gather.3.cloned.1.call-done = bf16[256,2048]{1,0:T(8,128)(2,1)} async-done(((bf16[256,512]{1,0:T(8,128)(2,1)}), bf16[256,2048]{1,0:T(8,128)(2,1)}) %all-gather.3.cloned.1.call-update) | async-done | bytes 1048592 | tf_op jit(solution)/shard_map/all_gather | solution.py:165
  114.7 0.0 all-gather.5.cloned.1.call-update
  114.7 4.5 all-to-all-start
  119.2 0.0 copy-done.1
  119.2 0.9 fusion.12
  120.1 0.0 copy-done.3
  120.1 0.1 add_dynamic-update-slice_fusion
  120.2 67.6 %psum.43 = f32[2048]{0:T(1024)S(1)} all-reduce(f32[2048]{0:T(1024)S(1)} %add_dynamic-update-slice_fusion), channel_id=1, replica_groups=mesh['ex'=8,'feat'=4] {'ex','feat'}, use_global_device_ids=true, to_apply=%region_1.0 | all-reduce | flops 2048 | bytes 16384 | tf_op jit(solution)/shard_map/psum | solution.py:187
  188.5 0.0 all-to-all-done
  188.5 2.8 copy.7
  191.3 0.0 all-gather.5.cloned.1.call-done
  191.3 24.9 %select_add_fusion.gram_ref = f32[2048,2048]{1,0:T(8,128)} fusion(bf16[2048,2048]{1,0:T(8,128)(2,1)} %all-gather.5.cloned.1.call-done), kind=kOutput, calls=%fused_computation | convolution fusion | flops 17192452096 | bytes 25165824 | tf_op jit(solution)/shard_map/dot_general | solution.py:167
  216.2 166.0 %shard_map.64 = (f32[2048,2048]{1,0:T(8,128)}, f32[2048,128]{1,0:T(8,128)S(1)}) custom-call(f32[2048,2048]{1,0:T(8,128)} %select_add_fusion.gram_ref), custom_call_target="tpu_custom_call" | custom-call | tf_op jit(solution)/shard_map/pallas_call | solution.py:123
  382.3 0.0 copy-start
  382.3 18.4 %convolution_bitcast_fusion.7 = f32[16,128,1]{1,2,0:T(1,128)S(1)} fusion(f32[2048,2048]{1,0:T(8,128)} %get-tuple-element.8, f32[2048,1]{0,1:T(1,128)S(1)} %bitcast.173), kind=kOutput, calls=%fused_computation.17 | convolution fusion | flops 50331648 | bytes 16793600 | tf_op jit(solution)/shard_map/dot_general | solution.py:175
  400.7 1.7 convolution_bitcast_fusion.3
  402.4 0.0 copy-done
  402.4 8.0 %fusion.13 = f32[1,2048]{1,0:T(1,128)S(1)} fusion(f32[2048,1]{0,1:T(1,128)S(1)} %convolution_bitcast_fusion.3, f32[2048,2048]{1,0:T(8,128)S(1)} %copy-done), kind=kOutput, calls=%fused_computation.55 | convolution fusion | flops 50331648 | bytes 16793600 | tf_op jit(solution)/shard_map/dot_general | solution.py:177
  410.4 0.9 convolution_bitcast_fusion.11
  411.3 1.7 fusion.14
  413.0 38.8 %psum.44 = f32[2048]{0:T(1024)S(1)} all-reduce(f32[2048]{0:T(1024)S(1)} %bitcast.175), channel_id=1, replica_groups=mesh['ex'=8,'feat'=4] {'ex','feat'}, use_global_device_ids=true, to_apply=%region_3.4 | all-reduce | flops 2048 | bytes 16384 | tf_op jit(solution)/shard_map/psum | solution.py:198
  451.8 0.6 multiply_reduce_fusion.7
  453.7 17.5 %convolution_bitcast_fusion.6 = f32[16,128,1]{1,2,0:T(1,128)S(1)} fusion(f32[2048,2048]{1,0:T(8,128)} %get-tuple-element.8, f32[2048,1]{0,1:T(1,128)S(1)} %bitcast.164), kind=kOutput, calls=%fused_computation.16 | convolution fusion | flops 50331648 | bytes 16793600 | tf_op jit(solution)/shard_map/dot_general | solution.py:175
  471.2 1.7 convolution_bitcast_fusion.2
  473.0 11.9 %fusion.15 = f32[1,2048]{1,0:T(1,128)S(1)} fusion(f32[2048,1]{0,1:T(1,128)S(1)} %convolution_bitcast_fusion.2, f32[2048,2048]{1,0:T(8,128)} %get-tuple-element.8), kind=kOutput, calls=%fused_computation.57 | convolution fusion | flops 50331648 | bytes 16793600 | tf_op jit(solution)/shard_map/dot_general | solution.py:177
  484.9 0.6 multiply_reduce_fusion.6
  486.8 0.9 convolution_bitcast_fusion.10
  487.7 1.7 fusion.16
  489.4 41.5 %psum.45 = f32[2048]{0:T(1024)S(1)} all-reduce(f32[2048]{0:T(1024)S(1)} %bitcast.176), channel_id=1, replica_groups=mesh['ex'=8,'feat'=4] {'ex','feat'}, use_global_device_ids=true, to_apply=%region_4.5 | all-reduce | flops 2048 | bytes 16384 | tf_op jit(solution)/shard_map/psum | solution.py:198
  530.9 0.6 multiply_reduce_fusion.5
  532.8 17.5 %convolution_bitcast_fusion.5 = f32[16,128,1]{1,2,0:T(1,128)S(1)} fusion(f32[2048,2048]{1,0:T(8,128)} %get-tuple-element.8, f32[2048,1]{0,1:T(1,128)S(1)} %bitcast.165), kind=kOutput, calls=%fused_computation.15 | convolution fusion | flops 50331648 | bytes 16793600 | tf_op jit(solution)/shard_map/dot_general | solution.py:175
  550.3 1.7 convolution_bitcast_fusion.1
  552.1 11.6 %fusion.17 = f32[1,2048]{1,0:T(1,128)S(1)} fusion(f32[2048,1]{0,1:T(1,128)S(1)} %convolution_bitcast_fusion.1, f32[2048,2048]{1,0:T(8,128)} %get-tuple-element.8), kind=kOutput, calls=%fused_computation.59 | convolution fusion | flops 50331648 | bytes 16793600 | tf_op jit(solution)/shard_map/dot_general | solution.py:177
  563.7 0.6 multiply_reduce_fusion.4
  565.6 0.9 convolution_bitcast_fusion.9
  566.5 1.7 fusion.18
  568.2 38.5 %psum.46 = f32[2048]{0:T(1024)S(1)} all-reduce(f32[2048]{0:T(1024)S(1)} %bitcast.177), channel_id=1, replica_groups=mesh['ex'=8,'feat'=4] {'ex','feat'}, use_global_device_ids=true, to_apply=%region_5.6 | all-reduce | flops 2048 | bytes 16384 | tf_op jit(solution)/shard_map/psum | solution.py:198
  606.8 0.6 multiply_reduce_fusion.3
  608.6 17.5 %convolution_bitcast_fusion.4 = f32[16,128,1]{1,2,0:T(1,128)S(1)} fusion(f32[2048,2048]{1,0:T(8,128)} %get-tuple-element.8, f32[2048,1]{0,1:T(1,128)S(1)} %bitcast.172), kind=kOutput, calls=%fused_computation.14 | convolution fusion | flops 50331648 | bytes 16793600 | tf_op jit(solution)/shard_map/dot_general | solution.py:175
  626.1 1.7 convolution_bitcast_fusion
  627.9 11.5 %fusion.19 = f32[1,2048]{1,0:T(1,128)S(1)} fusion(f32[2048,1]{0,1:T(1,128)S(1)} %convolution_bitcast_fusion, f32[2048,2048]{1,0:T(8,128)} %get-tuple-element.8), kind=kOutput, calls=%fused_computation.61 | convolution fusion | flops 50331648 | bytes 16793600 | tf_op jit(solution)/shard_map/dot_general | solution.py:177
  639.3 0.6 multiply_reduce_fusion.2
  641.2 0.9 convolution_bitcast_fusion.8
  642.1 1.7 fusion.20
  643.9 41.6 %psum.47 = f32[2048]{0:T(1024)S(1)} all-reduce(f32[2048]{0:T(1024)S(1)} %bitcast.174), channel_id=1, replica_groups=mesh['ex'=8,'feat'=4] {'ex','feat'}, use_global_device_ids=true, to_apply=%region_6.7 | all-reduce | flops 2048 | bytes 16384 | tf_op jit(solution)/shard_map/psum | solution.py:198
  685.4 0.7 multiply_reduce_fusion.1
  687.5 0.6 multiply_reduce_fusion
  688.8 0.7 multiply_add_fusion.7
  (10 shorter events, 0.1 us)
Async XLA Ops:
  6.5 78.2 %reduce-scatter.2.cloned.1.call-start = ((), (), s32[]{:S(2)}) async-start(), calls=%async_computation.2 | async-start | bytes 4718592 | tf_op jit(solution)/shard_map/reduce_scatter | solution.py:163
  26.3 1.4 copy-start.2
  35.0 84.2 %copy-start.1 = (bf16[2048,512]{1,0:T(8,128)(2,1)S(1)}, bf16[2048,512]{1,0:T(8,128)(2,1)}, u32[]{:S(2)}) copy-start(bf16[2048,512]{1,0:T(8,128)(2,1)} %param.6) | copy-start | bytes 6291460
  35.0 85.1 %copy-start.3 = (f32[512]{0:T(512)S(1)}, f32[512]{0:T(512)}, u32[]{:S(2)}) copy-start(f32[512]{0:T(512)} %param.7) | copy-start | bytes 6148
  35.1 79.6 %all-gather.3.cloned.1.call-start = ((), (), s32[]{:S(2)}) async-start(), calls=%async_computation.3 | async-start | bytes 1310720 | tf_op jit(solution)/shard_map/all_gather | solution.py:165
  86.6 104.7 %all-gather.5.cloned.1.call-start = ((), (), s32[]{:S(2)}) async-start(), calls=%async_computation.4 | async-start | bytes 9437184 | tf_op jit(solution)/shard_map/all_gather | solution.py:166
  114.7 73.8 %all-to-all-start = ((bf16[4,512,512]{2,1,0:T(8,128)(2,1)}), bf16[4,512,512]{2,1,0:T(8,128)(2,1)}, u32[]{:S(2)}, u32[]{:S(2)}) async-start(bf16[4,512,512]{2,1,0:T(8,128)(2,1)} %bitcast.156), calls=%async_computation.1 | async-start | bytes 4194304 | tf_op jit(solution)/shard_map/all_to_all | solution.py:184
  382.3 20.2 %copy-start = (f32[2048,2048]{1,0:T(8,128)S(1)}, f32[2048,2048]{1,0:T(8,128)}, u32[]{:S(2)}) copy-start(f32[2048,2048]{1,0:T(8,128)} %get-tuple-element.8) | copy-start | bytes 50331652
Sparse Core Ops, SparseCore 0:
  35.2 49.5 reduce-scatter.1
  86.7 27.9 all-gather.2
  116.7 54.3 all-gather.4

commit v2 on v1

v2 whole, which is shorter than its diff:
```python
import functools
import math

import jax
import jax.numpy as jnp
from jax import lax
from jax.experimental import pallas as pl
from jax.experimental.pallas import tpu as pltpu
from jax.sharding import PartitionSpec as P

D = 2048
ITERS = 4
REG = 0.02
BLOCK = 128
PIVOTS = 8
CHUNK = 256


def split(value):
    high = value.astype(jnp.bfloat16)
    low = (value - high.astype(jnp.float32)).astype(jnp.bfloat16)
    return high, low


def invert_block(block):
    tiles = BLOCK // PIVOTS
    lane = lax.broadcasted_iota(jnp.int32, (PIVOTS, BLOCK), 1)
    sub = lax.broadcasted_iota(jnp.int32, (PIVOTS, BLOCK), 0)
    shape = (PIVOTS, BLOCK)
    held = [block[t * PIVOTS : (t + 1) * PIVOTS, :] for t in range(tiles)]
    for step in range(tiles):
        first = step * PIVOTS
        rows = held[step]
        inside = (lane >= first) & (lane < first + PIVOTS)
        wide = [jnp.broadcast_to(rows[:, first + j : first + j + 1], shape) for j in range(PIVOTS)]
        cell = {}
        for j in range(PIVOTS):
            for i in range(j, PIVOTS):
                cell[i, j] = jnp.broadcast_to(wide[j][i : i + 1, :], shape)
        rows = jnp.where(inside, (lane - first == sub).astype(jnp.float32), rows)
        line = [jnp.broadcast_to(rows[i : i + 1, :], shape) for i in range(PIVOTS)]
        scaled = {}
        pairs = []
        for j in range(0, PIVOTS, 2):
            a, b, d = cell[j, j], cell[j + 1, j], cell[j + 1, j + 1]
            inverse = 1.0 / (a * d - b * b)
            pairs.append((a * inverse, b * inverse, d * inverse))
            for i in range(j + 2, PIVOTS):
                one, two = cell[i, j], cell[i, j + 1]
                scaled[i, j] = one * d - two * b
                scaled[i, j + 1] = two * a - one * b
            for i in range(j + 2, PIVOTS):
                for m in range(j + 2, i + 1):
                    product = scaled[i, j] * cell[m, j] + scaled[i, j + 1] * cell[m, j + 1]
                    cell[i, m] = cell[i, m] - product * inverse
            for i in range(j + 2, PIVOTS):
                scaled[i, j] = scaled[i, j] * inverse
                scaled[i, j + 1] = scaled[i, j + 1] * inverse
                line[i] = line[i] - (scaled[i, j] * line[j] + scaled[i, j + 1] * line[j + 1])
        for j in range(PIVOTS - 2, -1, -2):
            a, b, d = pairs[j // 2]
            one = line[j] * d - line[j + 1] * b
            two = line[j + 1] * a - line[j] * b
            for i in range(j + 2, PIVOTS):
                one = one - scaled[i, j] * line[i]
                two = two - scaled[i, j + 1] * line[i]
            line[j], line[j + 1] = one, two
        for t in [(step + 1 + t) % tiles for t in range(tiles - 1)]:
            tile = held[t]
            total = jnp.where(inside, 0.0, tile)
            for j in range(PIVOTS):
                total = total - tile[:, first + j : first + j + 1] * line[j]
            held[t] = total
        rows = line[0]
        for j in range(1, PIVOTS):
            rows = jnp.where(sub == j, line[j], rows)
        held[step] = rows
    return jnp.concatenate(held, axis=0)


def factor_kernel(gram_ref, work, inv_ref, right, diag, sem):
    size = gram_ref.shape[0]
    blocks = size // BLOCK
    copy = pltpu.make_async_copy(gram_ref, work, sem)
    copy.start()
    copy.wait()
    eye = (
        lax.broadcasted_iota(jnp.int32, (BLOCK, BLOCK), 0)
        == lax.broadcasted_iota(jnp.int32, (BLOCK, BLOCK), 1)
    ).astype(jnp.float32)

    def outer(k, _):
        here = pl.ds(pl.multiple_of(k * BLOCK, BLOCK), BLOCK)
        inverse = invert_block(work[here, here])
        inv_ref[here, :] = inverse
        inv_high, inv_low = split(inverse)
        diag[0:BLOCK, :] = inv_high
        diag[BLOCK : 2 * BLOCK, :] = inv_high
        diag[2 * BLOCK : 3 * BLOCK, :] = inv_low
        diag[3 * BLOCK : 4 * BLOCK, :] = inv_low
        work[here, here] = eye
        for c in range(size // CHUNK):
            cols = slice(c * CHUNK, (c + 1) * CHUNK)
            high, low = split(work[here, cols])
            right[0:BLOCK, cols] = high
            right[BLOCK : 2 * BLOCK, cols] = high
            right[2 * BLOCK : 3 * BLOCK, cols] = low
            right[3 * BLOCK : 4 * BLOCK, cols] = low

        def update(m, _):
            rows = pl.ds(pl.multiple_of(m * CHUNK, CHUNK), CHUNK)
            panel = work[rows, here]
            high, low = split(panel)
            wide = jnp.concatenate([high, low, high, low], axis=1)
            scaled = jnp.dot(wide, diag[...], preferred_element_type=jnp.float32)
            place = m * CHUNK + lax.broadcasted_iota(jnp.int32, (CHUNK, BLOCK), 0)
            later = place >= (k + 1) * BLOCK
            scaled = jnp.where(later, scaled, 0.0)
            work[rows, here] = jnp.where(later, 0.0, panel)
            high, low = split(scaled)
            wide = jnp.concatenate([high, low, high, low], axis=1)
            for c in range(size // CHUNK):
                cols = slice(c * CHUNK, (c + 1) * CHUNK)
                work[rows, cols] = work[rows, cols] - jnp.dot(
                    wide, right[:, cols], preferred_element_type=jnp.float32
                )
            return 0

        lax.fori_loop((k + 1) * BLOCK // CHUNK, size // CHUNK, update, 0)
        return 0

    lax.fori_loop(0, blocks, outer, 0)

    def clear(k, _):
        here = pl.ds(pl.multiple_of(k * BLOCK, BLOCK), BLOCK)
        for c in range(blocks):
            cols = slice(c * BLOCK, (c + 1) * BLOCK)
            work[here, cols] = jnp.where(c > k, 0.0, work[here, cols])
        return 0

    lax.fori_loop(0, blocks, clear, 0)


VMEM = pl.BlockSpec(memory_space=pltpu.VMEM)
LIMIT = 44 * 2**20


def factor(gram, interpret=False):
    size = gram.shape[0]
    return pl.pallas_call(
        factor_kernel,
        in_specs=[pl.BlockSpec(memory_space=pl.ANY)],
        out_specs=[VMEM, VMEM],
        out_shape=[
            pltpu.VMEM((size, size), jnp.float32),
            jax.ShapeDtypeStruct((size, BLOCK), jnp.float32),
        ],
        scratch_shapes=[
            pltpu.VMEM((4 * BLOCK, size), jnp.bfloat16),
            pltpu.VMEM((4 * BLOCK, BLOCK), jnp.bfloat16),
            pltpu.SemaphoreType.DMA,
        ],
        compiler_params=pltpu.CompilerParams(vmem_limit_bytes=LIMIT),
        interpret=interpret,
    )(gram)


GROUP = 4


def apply_inverse(lower, inverses, residual):
    size = residual.shape[1]
    blocks = size // BLOCK
    eye = lax.broadcasted_iota(jnp.int32, (BLOCK, BLOCK), 0) == lax.broadcasted_iota(
        jnp.int32, (BLOCK, BLOCK), 1
    )
    total = tuple(jnp.zeros((8, BLOCK), jnp.float32) for _ in range(blocks))
    for group in range(0, blocks, GROUP):
        used = min(group + GROUP, blocks)

        def one_block(k, total):
            here = pl.ds(pl.multiple_of(k * BLOCK, BLOCK), BLOCK)
            sums = jnp.zeros((BLOCK, BLOCK), jnp.float32)
            for c in range(used):
                cols = slice(c * BLOCK, (c + 1) * BLOCK)
                sums = sums + lower[here, cols] * residual[:, cols]
            column = jnp.sum(sums, axis=1, keepdims=True)
            row = jnp.sum(inverses[here, :] * column, axis=0, keepdims=True)
            column = jnp.sum(jnp.where(eye, row, 0.0), axis=1, keepdims=True)
            fresh = list(total)
            for c in range(used):
                cols = slice(c * BLOCK, (c + 1) * BLOCK)
                product = lower[here, cols] * column
                fresh[c] = fresh[c] + jnp.sum(product.reshape(BLOCK // 8, 8, BLOCK), axis=0)
            return tuple(fresh)

        total = lax.fori_loop(group, used, one_block, total)
    return jnp.concatenate([jnp.sum(t, axis=0, keepdims=True) for t in total], axis=1)


def curve(rows_ref, direction):
    count, size = rows_ref.shape
    blocks = size // BLOCK
    high = 16

    def step(i, total):
        here = pl.ds(pl.multiple_of(i * high, high), high)
        tile = rows_ref[here, :].astype(jnp.float32)
        sums = jnp.zeros((high, BLOCK), jnp.float32)
        for c in range(blocks):
            cols = slice(c * BLOCK, (c + 1) * BLOCK)
            sums = sums + tile[:, cols] * direction[:, cols]
        column = jnp.sum(sums, axis=1, keepdims=True)
        return tuple(
            total[c] + tile[:, c * BLOCK : (c + 1) * BLOCK] * column for c in range(blocks)
        )

    total = tuple(jnp.zeros((high, BLOCK), jnp.float32) for _ in range(blocks))
    total = lax.fori_loop(0, count // high, step, total, unroll=2)
    return jnp.concatenate([jnp.sum(t, axis=0, keepdims=True) for t in total], axis=1)


def dot(left, right):
    return jnp.sum(left * right, axis=1, keepdims=True)


def first_kernel(lower, inverses, rows, residual, direction, inner, curved):
    solved = apply_inverse(lower, inverses, residual[...])
    inner[...] = dot(residual[...], solved)
    direction[...] = solved
    curved[...] = curve(rows, direction)


def next_kernel(
    total_rows, lower, inverses, rows, pieces, solution, residual, direction, inner,
    solution_out, residual_out, direction_out, inner_out, curved_out,
):
    ahead = direction[...]
    curved = jnp.sum(pieces[...], axis=0, keepdims=True) / total_rows + (REG / D) * ahead
    size = inner[...] / dot(ahead, curved)
    solution_out[...] = solution[...] + size * ahead
    left = residual[...] - size * curved
    residual_out[...] = left
    solved = apply_inverse(lower, inverses, left)
    fresh = dot(left, solved)
    inner_out[...] = fresh
    direction_out[...] = solved + fresh / inner[...] * ahead
    curved_out[...] = curve(rows, direction_out)


def last_kernel(total_rows, pieces, solution, direction, inner, radius, out):
    ahead = direction[...]
    curved = jnp.sum(pieces[...], axis=0, keepdims=True) / total_rows + (REG / D) * ahead
    size = inner[...] / dot(ahead, curved)
    full = solution[...] + size * ahead
    length_sq = dot(full, full)
    scale = jnp.minimum(1.0, radius[...] * math.sqrt(D) / jnp.sqrt(length_sq + 1e-06))
    out[...] = scale * full


def call(kernel, shapes, args):
    return pl.pallas_call(
        kernel,
        in_specs=[VMEM] * len(args),
        out_specs=[VMEM] * len(shapes),
        out_shape=[jax.ShapeDtypeStruct(shape, jnp.float32) for shape in shapes],
        compiler_params=pltpu.CompilerParams(vmem_limit_bytes=LIMIT),
    )(*args)


def exchange(value, axis):
    count = lax.axis_size(axis)
    pieces = [value]
    for mask in range(1, count):
        pieces.append(lax.ppermute(value, axis, [(s, s ^ mask) for s in range(count)]))
    return pieces


def local(features, weights, labels, signs, samples, radius):
    highest = lax.Precision.HIGHEST
    row_count, feat_width = features.shape
    ex_count = lax.axis_size("ex")
    ex_index = lax.axis_index("ex")
    feat_index = lax.axis_index("feat")
    total_rows = row_count * ex_count
    sample_count = samples.shape[0]
    ridge = REG / D
    dense = features.astype(jnp.float32)
    margins = sum(exchange(jnp.dot(dense, weights, precision=highest), "feat"))
    probability = 1.0 / (1.0 + jnp.exp(-margins))
    curvature = probability * (1.0 - probability)
    weighted = (jnp.sqrt(curvature)[:, None] * dense).astype(jnp.bfloat16)
    signed = weighted * signs.astype(jnp.bfloat16)[:, None]
    places = ex_index * row_count + lax.iota(jnp.int32, row_count)
    odd = lax.population_count(samples[:, None] & places[None, :]) & 1
    table = (1 - 2 * odd).astype(jnp.bfloat16)
    mixed = jnp.dot(table, signed, preferred_element_type=jnp.float32)
    summed = lax.psum_scatter(mixed, "ex", scatter_dimension=0, tiled=True)
    sketch = (summed * (1.0 / math.sqrt(total_rows * sample_count))).astype(jnp.bfloat16)
    wide_sketch = lax.all_gather(sketch, "feat", axis=1, tiled=True)
    piece = lax.all_gather(wide_sketch, "ex", axis=0, tiled=True)
    gram = lax.dot_general(
        piece, piece, (((0,), (0,)), ((), ())), preferred_element_type=jnp.float32
    )
    gram = gram + ridge * jnp.eye(D, dtype=jnp.float32)
    lower, inverses = factor(gram)

    grad_part = jnp.dot(probability - labels.astype(jnp.float32), dense, precision=highest)
    gradient = lax.psum(grad_part, "ex") / total_rows + ridge * weights
    own_rows = lax.all_to_all(weighted, "feat", split_axis=0, concat_axis=1, tiled=True)
    residual = -lax.all_gather(gradient, "feat", axis=0, tiled=True)[None, :]

    def across(curved):
        return jnp.concatenate(exchange(lax.psum(curved, "ex"), "feat"), axis=0)

    row, one = (1, D), (1, 1)
    direction, inner, curved = call(
        first_kernel, [row, one, row], [lower, inverses, own_rows, residual]
    )
    solution = jnp.zeros(row, jnp.float32)
    following = functools.partial(next_kernel, total_rows)
    for _ in range(ITERS - 1):
        solution, residual, direction, inner, curved = call(
            following,
            [row, row, row, one, row],
            [lower, inverses, own_rows, across(curved), solution, residual, direction, inner],
        )
    (step,) = call(
        functools.partial(last_kernel, total_rows),
        [row],
        [across(curved), solution, direction, inner, radius[None, :]],
    )
    own = lax.dynamic_slice_in_dim(step[0], feat_index * feat_width, feat_width, 0)
    return weights + own


def solution(mesh):
    in_specs = (P("ex", "feat"), P("feat"), P("ex"), P("ex"), P(), P())
    out_specs = P("feat")
    return jax.shard_map(local, mesh=mesh, in_specs=in_specs, out_specs=out_specs, check_vma=False)
```

time: 703 us -> 483 us (0.69)
  blocking collectives: 242 us -> 101 us
  matrix products: 168 us -> 36.6 us
  Pallas kernels: 166 us -> 193 us
  starting transfers between devices: 4.57 us -> 27 us
  waiting for transfers between devices: 77.8 us -> 94.6 us
  between operations: 23.7 us -> 14 us
    psum x6 -> x5, blocking collectives: 242 us -> 62.9 us  [the longest x4 48.3 us: across(): return jnp.concatenate(exchange(lax.psum(curved, 'ex'), 'feat'), axis=0)]
    dot_general x21 -> x1, matrix products: 135 us -> 3.31 us  [local(): margins = sum(exchange(jnp.dot(dense, weights, precision=highest), 'feat'))]
    pallas_call x0 -> x5, Pallas kernels: none -> 53.8 us  [call(): pl.pallas_call(kernel, in_specs=[VMEM] * len(args), out_specs=[VMEM] * le...]
    all_gather x0 -> x1, blocking collectives: none -> 38.2 us  [local(): residual = -lax.all_gather(gradient, 'feat', axis=0, tiled=True)[None, :]]
    pallas_call x1, Pallas kernels: 166 us -> 139 us  [factor(): pl.pallas_call(factor_kernel, in_specs=[pl.BlockSpec(memory_space=pl.ANY)...]
    ppermute x0 -> x15, starting transfers between devices: none -> 22.5 us  [exchange(): lax.ppermute(value, axis, [(s, s ^ mask) for s in range(count)])]
    ppermute x0 -> x15, waiting for transfers between devices: none -> 16.8 us  [exchange(): lax.ppermute(value, axis, [(s, s ^ mask) for s in range(count)])]
    unnamed x8 -> x12, local copies, waits for them, and re-layouts: 0.67 us -> 8.31 us
  transfers between devices with their start and end apart: 4 -> 19, of which waited for: 2 -> 12; matrix products, arithmetic and copies ran while one was open for 1% -> 1% of each run, Pallas kernels for 0% -> 0%
where the time goes in v2:
time: 483 us; the launch traced here: 482 us
  Pallas kernels  193 us (40%)
  blocking collectives  101 us (21%)
  waiting for transfers between devices  94.6 us (20%)
  matrix products  36.6 us (8%)
  starting transfers between devices  27 us (6%)
  between operations  14 us (3%)
  local copies, waits for them, and re-layouts  10.2 us (2%)
  other arithmetic  6.01 us (1%)
    pallas_call x1, Pallas kernels, factor(): pl.pallas_call(factor_kernel, in_specs=[pl.BlockSpec(memory_space=pl.ANY)...  139 us
    pallas_call x5, Pallas kernels, call(): pl.pallas_call(kernel, in_specs=[VMEM] * len(args), out_specs=[VMEM] * le...  53.8 us
    reduce_scatter x1, waiting for transfers between devices, local(): summed = lax.psum_scatter(mixed, 'ex', scatter_dimension=0, tiled=True)  49.6 us
    psum x4, blocking collectives, across(): return jnp.concatenate(exchange(lax.psum(curved, 'ex'), 'feat'), axis=0)  48.3 us
    all_gather x1, blocking collectives, local(): residual = -lax.all_gather(gradient, 'feat', axis=0, tiled=True)[None, :]  38.2 us
    all_gather x1, waiting for transfers between devices, local(): wide_sketch = lax.all_gather(sketch, 'feat', axis=1, tiled=True)  28 us
    dot_general x1, matrix products, local(): lax.dot_general(piece, piece, (((0,), (0,)), ((), ())), preferred_element...  25 us
    ppermute x15, starting transfers between devices, exchange(): lax.ppermute(value, axis, [(s, s ^ mask) for s in range(count)])  22.5 us
  transfers between devices with their start and end apart: 19, of which 12 were waited for; matrix products, arithmetic and copies ran while one was open for 1% of the time, Pallas kernels for 0%

profile of v2, /device:TPU:0, one launch (start us, length us, event | category | flops | bytes accessed | tf_op | source)
XLA Modules:
  0.0 482.0 jit_solution(16113949651714930983)
XLA Ops:
  6.5 3.3 fusion.10
  9.8 3.0 collective-permute-start
  12.9 2.6 collective-permute-start.1
  15.5 0.0 collective-permute-start.2
  15.5 0.7 convert_element_type.22
  16.2 0.0 collective-permute-done
  16.2 1.2 collective-permute-done.1
  17.4 3.5 collective-permute-done.2
  20.9 0.7 convert_subtract_fusion
  21.6 2.0 multiply_convert_fusion
  23.7 1.3 copy-done.4
  25.0 7.3 %fusion = f32[2048,512]{1,0:T(8,128)} fusion(s32[2048]{0:T(1024)S(1)} %iota_add_fusion, s32[2048]{0:T(1024)} %param.10, bf16[2048,512]{1,0:T(8,128)(2,1)S(1)} %multiply_convert_fusion, bf16[2048]{0:T(1024)(128)(2,1)S(1)} %convert_element_type.22), kind=kOutput, calls=%fused_computation.3 | convolution fusion | flops 4321181696 | bytes 6311936 | tf_op jit(solution)/shard_map/dot_general | solution.py:297
  32.4 0.0 reduce-scatter.2.cloned.1.call-update
  32.4 0.0 all-gather.4.cloned.1.call-start
  32.5 49.6 %reduce-scatter.2.cloned.1.call-done = f32[256,512]{1,0:T(8,128)} async-done(((f32[2048,512]{1,0:T(8,128)}), f32[256,512]{1,0:T(8,128)}) %reduce-scatter.2.cloned.1.call-update) | async-done | bytes 524304 | tf_op jit(solution)/shard_map/reduce_scatter | solution.py:298
  82.1 1.8 multiply_convert_fusion.1
  83.9 0.0 all-gather.4.cloned.1.call-update
  83.9 0.0 all-gather.6.cloned.1.call-start
  83.9 28.0 %all-gather.4.cloned.1.call-done = bf16[256,2048]{1,0:T(8,128)(2,1)} async-done(((bf16[256,512]{1,0:T(8,128)(2,1)}), bf16[256,2048]{1,0:T(8,128)(2,1)}) %all-gather.4.cloned.1.call-update) | async-done | bytes 1048592 | tf_op jit(solution)/shard_map/all_gather | solution.py:300
  112.0 0.0 all-gather.6.cloned.1.call-update
  112.0 4.5 all-to-all-start
  116.5 0.9 fusion.11
  117.4 14.5 %psum.35 = f32[512]{0:T(512)S(1)} all-reduce(f32[512]{0:T(512)S(1)} %bitcast.32), channel_id=1, replica_groups=mesh['ex'=8,'feat'=4] {'ex'}, use_global_device_ids=true, to_apply=%region_1.0 | all-reduce | flops 512 | bytes 4096 | tf_op jit(solution)/shard_map/psum | solution.py:309
  131.9 38.2 %all-gather = f32[4,1,512]{2,1,0:T(1,128)S(1)} all-gather(f32[1,1,512]{2,1,0:T(1,128)S(1)} %bitcast.33), channel_id=1, replica_groups=mesh['ex'=8,'feat'=4] {'feat'}, dimensions={0}, use_global_device_ids=true | all-gather | bytes 10240 | tf_op jit(solution)/shard_map/all_gather | solution.py:311
  170.1 0.0 all-to-all-done
  170.1 1.9 copy.9
  172.0 0.0 all-gather.6.cloned.1.call-done
  172.0 25.0 %select_add_fusion.gram_ref = f32[2048,2048]{1,0:T(8,128)} fusion(bf16[2048,2048]{1,0:T(8,128)(2,1)} %all-gather.6.cloned.1.call-done), kind=kOutput, calls=%fused_computation | convolution fusion | flops 17192452096 | bytes 25165824 | tf_op jit(solution)/shard_map/dot_general | solution.py:302
  197.0 138.8 %shard_map.64 = (f32[2048,2048]{1,0:T(8,128)S(1)}, f32[2048,128]{1,0:T(8,128)}) custom-call(f32[2048,2048]{1,0:T(8,128)} %select_add_fusion.gram_ref), custom_call_target="tpu_custom_call" | custom-call | tf_op jit(solution)/shard_map/pallas_call | solution.py:150
  335.9 5.7 %copy-done = f32[2048,2048]{1,0:T(8,128)} copy-done((f32[2048,2048]{1,0:T(8,128)}, f32[2048,2048]{1,0:T(8,128)S(1)}, u32[]{:S(2)}) %copy-start) | copy-done | bytes 16777240
  341.6 1.2 copy-done.1
  342.8 12.5 %shard_map.65 = (f32[1,2048]{1,0:T(1,128)S(1)}, f32[1,1]{1,0:T(1,128)}, f32[1,2048]{1,0:T(1,128)S(1)}) custom-call(f32[2048,2048]{1,0:T(8,128)} %copy-done, f32[2048,128]{1,0:T(8,128)S(1)} %copy-done.1, bf16[512,2048]{1,0:T(8,128)(2,1)S(1)} %bitcast.19, f32[1,2048]{1,0:T(1,128)S(1)} %bitcast.23), custom_call_target="tpu_custom_call" | custom-call | tf_op jit(solution)/shard_map/pallas_call | solution.py:262
  355.4 12.1 %psum.36 = f32[1,2048]{1,0:T(1,128)S(1)} all-reduce(f32[1,2048]{1,0:T(1,128)S(1)} %get-tuple-element.26), channel_id=1, replica_groups=mesh['ex'=8,'feat'=4] {'ex'}, use_global_device_ids=true, to_apply=%region_2.0 | all-reduce | flops 2048 | bytes 16384 | tf_op jit(solution)/shard_map/psum | solution.py:314
  367.4 0.1 collective-permute-start.3
  367.5 1.2 collective-permute-start.4
  368.7 3.1 collective-permute-start.5
  371.9 0.0 collective-permute-done.3
  371.9 0.4 collective-permute-done.4
  372.3 1.9 collective-permute-done.5
  374.2 13.4 %shard_map.66 = (f32[1,2048]{1,0:T(1,128)S(1)}, f32[1,2048]{1,0:T(1,128)S(1)}, f32[1,2048]{1,0:T(1,128)S(1)}, f32[1,1]{1,0:T(1,128)}, f32[1,2048]{1,0:T(1,128)S(1)}) custom-call(f32[2048,2048]{1,0:T(8,128)} %copy-done, f32[2048,128]{1,0:T(8,128)S(1)} %copy-done.2, bf16[512,2048]{1,0:T(8,128)(2,1)S(1)} %bitcast.20, f32[4,2048]{1,0:T(4,128)S(1)} %pad_maximum_fusion.pieces, ...), custom_call_target="tpu_custom_call" | custom-call | tf_op jit(solution)/shard_map/pallas_call | solution.py:262
  387.7 12.2 %psum.37 = f32[1,2048]{1,0:T(1,128)S(1)} all-reduce(f32[1,2048]{1,0:T(1,128)S(1)} %get-tuple-element.29), channel_id=1, replica_groups=mesh['ex'=8,'feat'=4] {'ex'}, use_global_device_ids=true, to_apply=%region_3.0 | all-reduce | flops 2048 | bytes 16384 | tf_op jit(solution)/shard_map/psum | solution.py:314
  399.9 0.1 collective-permute-start.6
  400.0 3.7 collective-permute-start.7
  403.7 0.7 collective-permute-start.8
  404.4 0.0 collective-permute-done.6
  404.4 0.9 collective-permute-done.7
  405.3 3.8 collective-permute-done.8
  409.2 13.4 %shard_map.67 = (f32[1,2048]{1,0:T(1,128)S(1)}, f32[1,2048]{1,0:T(1,128)S(1)}, f32[1,2048]{1,0:T(1,128)S(1)}, f32[1,1]{1,0:T(1,128)}, f32[1,2048]{1,0:T(1,128)S(1)}) custom-call(f32[2048,2048]{1,0:T(8,128)} %copy-done, f32[2048,128]{1,0:T(8,128)S(1)} %copy-done.2, bf16[512,2048]{1,0:T(8,128)(2,1)S(1)} %bitcast.21, f32[4,2048]{1,0:T(4,128)S(1)} %pad_maximum_fusion.1.pieces, ...), custom_call_target="tpu_custom_call" | custom-call | tf_op jit(solution)/shard_map/pallas_call | solution.py:262
  422.6 12.0 %psum.38 = f32[1,2048]{1,0:T(1,128)S(1)} all-reduce(f32[1,2048]{1,0:T(1,128)S(1)} %get-tuple-element.34), channel_id=1, replica_groups=mesh['ex'=8,'feat'=4] {'ex'}, use_global_device_ids=true, to_apply=%region_4.0 | all-reduce | flops 2048 | bytes 16384 | tf_op jit(solution)/shard_map/psum | solution.py:314
  434.6 0.1 collective-permute-start.10
  434.7 0.7 collective-permute-start.11
  435.5 2.7 collective-permute-start.9
  438.2 1.1 collective-permute-done.10
  439.2 1.0 collective-permute-done.11
  440.2 0.0 collective-permute-done.9
  440.3 13.5 %shard_map.68 = (f32[1,2048]{1,0:T(1,128)S(1)}, f32[1,2048]{1,0:T(1,128)}, f32[1,2048]{1,0:T(1,128)S(1)}, f32[1,1]{1,0:T(1,128)}, f32[1,2048]{1,0:T(1,128)S(1)}) custom-call(f32[2048,2048]{1,0:T(8,128)} %copy-done, f32[2048,128]{1,0:T(8,128)S(1)} %copy-done.2, bf16[512,2048]{1,0:T(8,128)(2,1)S(1)} %bitcast.22, f32[4,2048]{1,0:T(4,128)S(1)} %pad_maximum_fusion.2.pieces, ...), custom_call_target="tpu_custom_call" | custom-call | tf_op jit(solution)/shard_map/pallas_call | solution.py:262
  453.8 12.0 %psum.39 = f32[1,2048]{1,0:T(1,128)S(1)} all-reduce(f32[1,2048]{1,0:T(1,128)S(1)} %get-tuple-element.39), channel_id=1, replica_groups=mesh['ex'=8,'feat'=4] {'ex'}, use_global_device_ids=true, to_apply=%region_5.0 | all-reduce | flops 2048 | bytes 16384 | tf_op jit(solution)/shard_map/psum | solution.py:314
  465.8 1.7 collective-permute-start.12
  467.5 1.0 collective-permute-start.13
  468.4 1.8 collective-permute-start.14
  470.9 1.1 collective-permute-done.13
  472.0 1.9 collective-permute-done.14
  473.9 1.0 shard_map.69
  474.9 0.6 add.55
  (21 shorter events, 0.2 us)
Async XLA Ops:
  6.5 75.6 %reduce-scatter.2.cloned.1.call-start = ((), (), s32[]{:S(2)}) async-start(), calls=%async_computation.2 | async-start | bytes 4718592 | tf_op jit(solution)/shard_map/reduce_scatter | solution.py:298
  9.8 6.3 %collective-permute-start = (f32[2048]{0:T(1024)S(1)}, f32[2048]{0:T(1024)S(1)}, u32[]{:S(2)}, u32[]{:S(2)}) collective-permute-start(f32[2048]{0:T(1024)S(1)} %bitcast.27), channel_id=1, source_target_pairs={{0,1},{1,0},{2,3},{3,2},{4,5},{5,4},{6,7},{7,6},{8,9},{9,8},{10,11... | collective-permute-start | bytes 24584 | tf_op jit(solution)/shard_map/ppermute | solution.py:275
  12.9 4.5 collective-permute-start.1
  15.5 5.4 %collective-permute-start.2 = (f32[2048]{0:T(1024)S(1)}, f32[2048]{0:T(1024)S(1)}, u32[]{:S(2)}, u32[]{:S(2)}) collective-permute-start(f32[2048]{0:T(1024)S(1)} %bitcast.29), channel_id=1, source_target_pairs={{0,3},{1,2},{2,1},{3,0},{4,7},{5,6},{6,5},{7,4},{8,11},{9,10},{10,... | collective-permute-start | bytes 24584 | tf_op jit(solution)/shard_map/ppermute | solution.py:275
  23.7 1.4 copy-start.4
  32.4 84.1 %copy-start.3 = (bf16[2048,512]{1,0:T(8,128)(2,1)S(1)}, bf16[2048,512]{1,0:T(8,128)(2,1)}, u32[]{:S(2)}) copy-start(bf16[2048,512]{1,0:T(8,128)(2,1)} %param.6) | copy-start | bytes 6291460
  32.4 99.6 %copy-start.5 = (f32[512]{0:T(512)S(1)}, f32[512]{0:T(512)}, u32[]{:S(2)}) copy-start(f32[512]{0:T(512)} %param.7) | copy-start | bytes 6148
  32.4 79.6 %all-gather.4.cloned.1.call-start = ((), (), s32[]{:S(2)}) async-start(), calls=%async_computation.3 | async-start | bytes 1310720 | tf_op jit(solution)/shard_map/all_gather | solution.py:300
  83.9 88.1 %all-gather.6.cloned.1.call-start = ((), (), s32[]{:S(2)}) async-start(), calls=%async_computation.4 | async-start | bytes 9437184 | tf_op jit(solution)/shard_map/all_gather | solution.py:301
  112.0 58.1 %all-to-all-start = ((bf16[4,512,512]{2,1,0:T(8,128)(2,1)}), bf16[4,512,512]{2,1,0:T(8,128)(2,1)}, u32[]{:S(2)}, u32[]{:S(2)}) async-start(bf16[4,512,512]{2,1,0:T(8,128)(2,1)} %bitcast.25), calls=%async_computation.1 | async-start | bytes 4194304 | tf_op jit(solution)/shard_map/all_to_all | solution.py:310
  335.9 5.7 %copy-start = (f32[2048,2048]{1,0:T(8,128)}, f32[2048,2048]{1,0:T(8,128)S(1)}, u32[]{:S(2)}) copy-start(f32[2048,2048]{1,0:T(8,128)S(1)} %get-tuple-element.24.lower) | copy-start | bytes 50331652
  341.6 1.2 copy-start.1
  342.8 31.4 %copy-start.2 = (f32[2048,128]{1,0:T(8,128)S(1)}, f32[2048,128]{1,0:T(8,128)}, u32[]{:S(2)}) copy-start(f32[2048,128]{1,0:T(8,128)} %get-tuple-element.25.inverses) | copy-start | bytes 3145732
  367.4 4.5 collective-permute-start.3
  367.5 4.8 collective-permute-start.4
  368.7 5.4 %collective-permute-start.5 = (f32[1,2048]{1,0:T(1,128)S(1)}, f32[1,2048]{1,0:T(1,128)S(1)}, u32[]{:S(2)}, u32[]{:S(2)}) collective-permute-start(f32[1,2048]{1,0:T(1,128)S(1)} %psum.36), channel_id=1, source_target_pairs={{0,3},{1,2},{2,1},{3,0},{4,7},{5,6},{6,5},{7,4},{8,11},{9,10},{10,... | collective-permute-start | bytes 24584 | tf_op jit(solution)/shard_map/ppermute | solution.py:275
  399.9 4.5 collective-permute-start.6
  400.0 5.3 %collective-permute-start.7 = (f32[1,2048]{1,0:T(1,128)S(1)}, f32[1,2048]{1,0:T(1,128)S(1)}, u32[]{:S(2)}, u32[]{:S(2)}) collective-permute-start(f32[1,2048]{1,0:T(1,128)S(1)} %psum.37), channel_id=1, source_target_pairs={{0,2},{1,3},{2,0},{3,1},{4,6},{5,7},{6,4},{7,5},{8,10},{9,11},{10,... | collective-permute-start | bytes 24584 | tf_op jit(solution)/shard_map/ppermute | solution.py:275
  403.7 5.4 %collective-permute-start.8 = (f32[1,2048]{1,0:T(1,128)S(1)}, f32[1,2048]{1,0:T(1,128)S(1)}, u32[]{:S(2)}, u32[]{:S(2)}) collective-permute-start(f32[1,2048]{1,0:T(1,128)S(1)} %psum.37), channel_id=1, source_target_pairs={{0,3},{1,2},{2,1},{3,0},{4,7},{5,6},{6,5},{7,4},{8,11},{9,10},{10,... | collective-permute-start | bytes 24584 | tf_op jit(solution)/shard_map/ppermute | solution.py:275
  434.6 4.6 collective-permute-start.10
  434.7 5.5 %collective-permute-start.11 = (f32[1,2048]{1,0:T(1,128)S(1)}, f32[1,2048]{1,0:T(1,128)S(1)}, u32[]{:S(2)}, u32[]{:S(2)}) collective-permute-start(f32[1,2048]{1,0:T(1,128)S(1)} %psum.38), channel_id=1, source_target_pairs={{0,3},{1,2},{2,1},{3,0},{4,7},{5,6},{6,5},{7,4},{8,11},{9,10},{10,... | collective-permute-start | bytes 24584 | tf_op jit(solution)/shard_map/ppermute | solution.py:275
  435.5 4.8 collective-permute-start.9
  465.8 5.1 %collective-permute-start.12 = (f32[1,2048]{1,0:T(1,128)S(1)}, f32[1,2048]{1,0:T(1,128)S(1)}, u32[]{:S(2)}, u32[]{:S(2)}) collective-permute-start(f32[1,2048]{1,0:T(1,128)S(1)} %psum.39), channel_id=1, source_target_pairs={{0,1},{1,0},{2,3},{3,2},{4,5},{5,4},{6,7},{7,6},{8,9},{9,8},{10,11... | collective-permute-start | bytes 24584 | tf_op jit(solution)/shard_map/ppermute | solution.py:275
  467.5 4.5 collective-permute-start.13
  468.4 5.4 %collective-permute-start.14 = (f32[1,2048]{1,0:T(1,128)S(1)}, f32[1,2048]{1,0:T(1,128)S(1)}, u32[]{:S(2)}, u32[]{:S(2)}) collective-permute-start(f32[1,2048]{1,0:T(1,128)S(1)} %psum.39), channel_id=1, source_target_pairs={{0,3},{1,2},{2,1},{3,0},{4,7},{5,6},{6,5},{7,4},{8,11},{9,10},{10,... | collective-permute-start | bytes 24584 | tf_op jit(solution)/shard_map/ppermute | solution.py:275
Sparse Core Ops, SparseCore 0:
  32.5 49.5 reduce-scatter.1
  84.0 27.9 all-gather.3
  114.0 53.9 all-gather.5

commit v3 on v2

--- a/solution.py
+++ b/solution.py
@@ -78,12 +78,41 @@
     return jnp.concatenate(held, axis=0)
 
 
-def factor_kernel(gram_ref, work, inv_ref, right, diag, sem):
-    size = gram_ref.shape[0]
+def factor_kernel(pieces, work, inv_ref, sketch, right, diag, sem):
+    size = work.shape[0]
     blocks = size // BLOCK
-    copy = pltpu.make_async_copy(gram_ref, work, sem)
-    copy.start()
-    copy.wait()
+    feat_count = pieces.shape[1]
+    width = size // feat_count
+    copies = [
+        pltpu.make_async_copy(
+            pieces.at[:, f], sketch.at[:, :, f * width : (f + 1) * width], sem.at[f]
+        )
+        for f in range(feat_count)
+    ]
+    for copy in copies:
+        copy.start()
+    for copy in copies:
+        copy.wait()
+    samples = sketch.shape[0] * sketch.shape[1]
+
+    def gram(m, _):
+        start = pl.multiple_of(m * CHUNK, CHUNK)
+        here = pl.ds(start, CHUNK)
+        mine = sketch[:, :, here].reshape(samples, CHUNK)
+        for c in range(size // CHUNK):
+            cols = slice(c * CHUNK, (c + 1) * CHUNK)
+            product = lax.dot_general(
+                mine,
+                sketch[:, :, cols].reshape(samples, CHUNK),
+                (((0,), (0,)), ((), ())),
+                preferred_element_type=jnp.float32,
+            )
+            row = start + lax.broadcasted_iota(jnp.int32, product.shape, 0)
+            col = c * CHUNK + lax.broadcasted_iota(jnp.int32, product.shape, 1)
+            work[here, cols] = jnp.where(row == col, product + REG / D, product)
+        return 0
+
+    lax.fori_loop(0, size // CHUNK, gram, 0)
     eye = (
         lax.broadcasted_iota(jnp.int32, (BLOCK, BLOCK), 0)
         == lax.broadcasted_iota(jnp.int32, (BLOCK, BLOCK), 1)
@@ -142,59 +171,70 @@
 
 
 VMEM = pl.BlockSpec(memory_space=pltpu.VMEM)
-LIMIT = 44 * 2**20
-
-
-def factor(gram, interpret=False):
-    size = gram.shape[0]
+
+
+def factor(pieces, interpret=False):
+    ex_count, feat_count, rows, width = pieces.shape
+    size = feat_count * width
     return pl.pallas_call(
         factor_kernel,
         in_specs=[pl.BlockSpec(memory_space=pl.ANY)],
         out_specs=[VMEM, VMEM],
         out_shape=[
             pltpu.VMEM((size, size), jnp.float32),
-            jax.ShapeDtypeStruct((size, BLOCK), jnp.float32),
+            pltpu.VMEM((size, BLOCK), jnp.float32),
         ],
         scratch_shapes=[
+            pltpu.VMEM((ex_count, rows, size), jnp.bfloat16),
             pltpu.VMEM((4 * BLOCK, size), jnp.bfloat16),
             pltpu.VMEM((4 * BLOCK, BLOCK), jnp.bfloat16),
-            pltpu.SemaphoreType.DMA,
+            pltpu.SemaphoreType.DMA((feat_count,)),
         ],
-        compiler_params=pltpu.CompilerParams(vmem_limit_bytes=LIMIT),
+        compiler_params=pltpu.CompilerParams(vmem_limit_bytes=36 * 2**20),
         interpret=interpret,
-    )(gram)
+    )(pieces)
 
 
 GROUP = 4
 
 
-def apply_inverse(lower, inverses, residual):
+def apply_inverse(lower, inverses, residual, column):
     size = residual.shape[1]
     blocks = size // BLOCK
     eye = lax.broadcasted_iota(jnp.int32, (BLOCK, BLOCK), 0) == lax.broadcasted_iota(
         jnp.int32, (BLOCK, BLOCK), 1
     )
-    total = tuple(jnp.zeros((8, BLOCK), jnp.float32) for _ in range(blocks))
     for group in range(0, blocks, GROUP):
-        used = min(group + GROUP, blocks)
-
-        def one_block(k, total):
+        used = group + GROUP
+
+        def down(k, _):
             here = pl.ds(pl.multiple_of(k * BLOCK, BLOCK), BLOCK)
             sums = jnp.zeros((BLOCK, BLOCK), jnp.float32)
             for c in range(used):
                 cols = slice(c * BLOCK, (c + 1) * BLOCK)
                 sums = sums + lower[here, cols] * residual[:, cols]
-            column = jnp.sum(sums, axis=1, keepdims=True)
-            row = jnp.sum(inverses[here, :] * column, axis=0, keepdims=True)
-            column = jnp.sum(jnp.where(eye, row, 0.0), axis=1, keepdims=True)
+            middle = jnp.sum(sums, axis=1, keepdims=True)
+            row = jnp.sum(inverses[here, :] * middle, axis=0, keepdims=True)
+            middle = jnp.sum(jnp.where(eye, row, 0.0), axis=1, keepdims=True)
+            column[here, :] = jnp.broadcast_to(middle, (BLOCK, BLOCK))
+            return 0
+
+        lax.fori_loop(group, used, down, 0, unroll=True)
+    total = tuple(jnp.zeros((8, BLOCK), jnp.float32) for _ in range(blocks))
+    for group in range(0, blocks, GROUP):
+        used = group + GROUP
+
+        def up(t, total):
+            here = pl.ds(pl.multiple_of(t * 32, 32), 32)
+            middle = column[here, :]
             fresh = list(total)
             for c in range(used):
                 cols = slice(c * BLOCK, (c + 1) * BLOCK)
-                product = lower[here, cols] * column
-                fresh[c] = fresh[c] + jnp.sum(product.reshape(BLOCK // 8, 8, BLOCK), axis=0)
+                product = lower[here, cols] * middle
+                fresh[c] = fresh[c] + jnp.sum(product.reshape(4, 8, BLOCK), axis=0)
             return tuple(fresh)
 
-        total = lax.fori_loop(group, used, one_block, total)
+        total = lax.fori_loop(group * BLOCK // 32, used * BLOCK // 32, up, total)
     return jnp.concatenate([jnp.sum(t, axis=0, keepdims=True) for t in total], axis=1)
 
 
@@ -211,12 +251,14 @@
             cols = slice(c * BLOCK, (c + 1) * BLOCK)
             sums = sums + tile[:, cols] * direction[:, cols]
         column = jnp.sum(sums, axis=1, keepdims=True)
-        return tuple(
-            total[c] + tile[:, c * BLOCK : (c + 1) * BLOCK] * column for c in range(blocks)
-        )
-
-    total = tuple(jnp.zeros((high, BLOCK), jnp.float32) for _ in range(blocks))
-    total = lax.fori_loop(0, count // high, step, total, unroll=2)
+        fresh = list(total)
+        for c in range(blocks):
+            product = tile[:, c * BLOCK : (c + 1) * BLOCK] * column
+            fresh[c] = fresh[c] + (product[:8] + product[8:])
+        return tuple(fresh)
+
+    total = tuple(jnp.zeros((8, BLOCK), jnp.float32) for _ in range(blocks))
+    total = lax.fori_loop(0, count // high, step, total, unroll=4)
     return jnp.concatenate([jnp.sum(t, axis=0, keepdims=True) for t in total], axis=1)
 
 
@@ -224,33 +266,33 @@
     return jnp.sum(left * right, axis=1, keepdims=True)
 
 
-def first_kernel(lower, inverses, rows, residual, direction, inner, curved):
-    solved = apply_inverse(lower, inverses, residual[...])
+def first_kernel(lower, inverses, rows, residual, direction, inner, curved, column):
+    solved = apply_inverse(lower, inverses, residual[...], column)
     inner[...] = dot(residual[...], solved)
     direction[...] = solved
     curved[...] = curve(rows, direction)
 
 
 def next_kernel(
-    total_rows, lower, inverses, rows, pieces, solution, residual, direction, inner,
-    solution_out, residual_out, direction_out, inner_out, curved_out,
+    total_rows, lower, inverses, rows, sums, solution, residual, direction, inner,
+    solution_out, residual_out, direction_out, inner_out, curved_out, column,
 ):
     ahead = direction[...]
-    curved = jnp.sum(pieces[...], axis=0, keepdims=True) / total_rows + (REG / D) * ahead
+    curved = sums[...] / total_rows + (REG / D) * ahead
     size = inner[...] / dot(ahead, curved)
     solution_out[...] = solution[...] + size * ahead
     left = residual[...] - size * curved
     residual_out[...] = left
-    solved = apply_inverse(lower, inverses, left)
+    solved = apply_inverse(lower, inverses, left, column)
     fresh = dot(left, solved)
     inner_out[...] = fresh
     direction_out[...] = solved + fresh / inner[...] * ahead
     curved_out[...] = curve(rows, direction_out)
 
 
-def last_kernel(total_rows, pieces, solution, direction, inner, radius, out):
+def last_kernel(total_rows, sums, solution, direction, inner, radius, out):
     ahead = direction[...]
-    curved = jnp.sum(pieces[...], axis=0, keepdims=True) / total_rows + (REG / D) * ahead
+    curved = sums[...] / total_rows + (REG / D) * ahead
     size = inner[...] / dot(ahead, curved)
     full = solution[...] + size * ahead
     length_sq = dot(full, full)
@@ -258,13 +300,18 @@
     out[...] = scale * full
 
 
-def call(kernel, shapes, args):
+def call(kernel, shapes, args, scratch=()):
+    args = list(args)
+    for place, value in enumerate(args):
+        if value.size >= BLOCK * D:
+            args[place] = pltpu.with_memory_space_constraint(value, pltpu.VMEM)
     return pl.pallas_call(
         kernel,
         in_specs=[VMEM] * len(args),
         out_specs=[VMEM] * len(shapes),
         out_shape=[jax.ShapeDtypeStruct(shape, jnp.float32) for shape in shapes],
-        compiler_params=pltpu.CompilerParams(vmem_limit_bytes=LIMIT),
+        scratch_shapes=scratch,
+        compiler_params=pltpu.CompilerParams(vmem_limit_bytes=8 * 2**20),
     )(*args)
 
 
@@ -276,15 +323,25 @@
     return pieces
 
 
+def butterfly(value):
+    for axis in ("ex", "feat"):
+        count = lax.axis_size(axis)
+        mask = 1
+        while mask < count:
+            value = value + lax.ppermute(value, axis, [(s, s ^ mask) for s in range(count)])
+            mask = mask * 2
+    return value
+
+
 def local(features, weights, labels, signs, samples, radius):
     highest = lax.Precision.HIGHEST
     row_count, feat_width = features.shape
     ex_count = lax.axis_size("ex")
     ex_index = lax.axis_index("ex")
+    feat_count = lax.axis_size("feat")
     feat_index = lax.axis_index("feat")
     total_rows = row_count * ex_count
     sample_count = samples.shape[0]
-    ridge = REG / D
     dense = features.astype(jnp.float32)
     margins = sum(exchange(jnp.dot(dense, weights, precision=highest), "feat"))
     probability = 1.0 / (1.0 + jnp.exp(-margins))
@@ -297,25 +354,18 @@
     mixed = jnp.dot(table, signed, preferred_element_type=jnp.float32)
     summed = lax.psum_scatter(mixed, "ex", scatter_dimension=0, tiled=True)
     sketch = (summed * (1.0 / math.sqrt(total_rows * sample_count))).astype(jnp.bfloat16)
-    wide_sketch = lax.all_gather(sketch, "feat", axis=1, tiled=True)
-    piece = lax.all_gather(wide_sketch, "ex", axis=0, tiled=True)
-    gram = lax.dot_general(
-        piece, piece, (((0,), (0,)), ((), ())), preferred_element_type=jnp.float32
-    )
-    gram = gram + ridge * jnp.eye(D, dtype=jnp.float32)
-    lower, inverses = factor(gram)
+    pieces = lax.all_gather(sketch, ("ex", "feat"), axis=0)
+    lower, inverses = factor(pieces.reshape(ex_count, feat_count, *sketch.shape))
 
     grad_part = jnp.dot(probability - labels.astype(jnp.float32), dense, precision=highest)
-    gradient = lax.psum(grad_part, "ex") / total_rows + ridge * weights
+    gradient = lax.psum(grad_part, "ex") / total_rows + (REG / D) * weights
     own_rows = lax.all_to_all(weighted, "feat", split_axis=0, concat_axis=1, tiled=True)
     residual = -lax.all_gather(gradient, "feat", axis=0, tiled=True)[None, :]
 
-    def across(curved):
-        return jnp.concatenate(exchange(lax.psum(curved, "ex"), "feat"), axis=0)
-
     row, one = (1, D), (1, 1)
+    scratch = [pltpu.VMEM((D, BLOCK), jnp.float32)]
     direction, inner, curved = call(
-        first_kernel, [row, one, row], [lower, inverses, own_rows, residual]
+        first_kernel, [row, one, row], [lower, inverses, own_rows, residual], scratch
     )
     solution = jnp.zeros(row, jnp.float32)
     following = functools.partial(next_kernel, total_rows)
@@ -323,12 +373,13 @@
         solution, residual, direction, inner, curved = call(
             following,
             [row, row, row, one, row],
-            [lower, inverses, own_rows, across(curved), solution, residual, direction, inner],
+            [lower, inverses, own_rows, butterfly(curved), solution, residual, direction, inner],
+            scratch,
         )
     (step,) = call(
         functools.partial(last_kernel, total_rows),
         [row],
-        [across(curved), solution, direction, inner, radius[None, :]],
+        [butterfly(curved), solution, direction, inner, radius[None, :]],
     )
     own = lax.dynamic_slice_in_dim(step[0], feat_index * feat_width, feat_width, 0)
     return weights + own

time: 483 us -> 437 us (0.905)
  blocking collectives: 101 us -> 68.5 us
  waiting for transfers between devices: 94.6 us -> 122 us
  matrix products: 36.6 us -> 10.9 us
  Pallas kernels: 193 us -> 174 us
  starting transfers between devices: 27 us -> 37.7 us
  local copies, waits for them, and re-layouts: 10.2 us -> 3.37 us
    psum x5 -> x1, blocking collectives: 62.9 us -> 13.3 us  [local(): gradient = lax.psum(grad_part, 'ex') / total_rows + REG / D * weights]
    ppermute x0 -> x20, waiting for transfers between devices: none -> 39.6 us  [butterfly(): lax.ppermute(value, axis, [(s, s ^ mask) for s in range(count)])]
    pallas_call x5, Pallas kernels: 53.8 us -> 20.4 us  [call(): pl.pallas_call(kernel, in_specs=[VMEM] * len(args), out_specs=[VMEM] * le...]
    ppermute x0 -> x20, starting transfers between devices: none -> 27.5 us  [butterfly(): lax.ppermute(value, axis, [(s, s ^ mask) for s in range(count)])]
    dot_general x1 -> x0, matrix products: 25 us -> none  [local(): lax.dot_general(piece, piece, (((0,), (0,)), ((), ())), preferred_element...]
    all_gather x1, blocking collectives: 38.2 us -> 55.2 us  [local(): residual = -lax.all_gather(gradient, 'feat', axis=0, tiled=True)[None, :]]
    ppermute x15 -> x3, starting transfers between devices: 22.5 us -> 5.62 us  [exchange(): lax.ppermute(value, axis, [(s, s ^ mask) for s in range(count)])]
    pallas_call x1, Pallas kernels: 139 us -> 154 us  [factor(): pl.pallas_call(factor_kernel, in_specs=[pl.BlockSpec(memory_space=pl.ANY)...]
  transfers between devices with their start and end apart: 19 -> 26, of which waited for: 12 -> 24; matrix products, arithmetic and copies ran while one was open for 1% -> 1% of each run, Pallas kernels for 0% -> 0%
where the time goes in v3:
time: 437 us
  Pallas kernels  174 us (40%)
  waiting for transfers between devices  122 us (28%)
  blocking collectives  68.5 us (16%)
  starting transfers between devices  37.7 us (9%)
  between operations  14.2 us (3%)
  matrix products  10.9 us (2%)
  other arithmetic  6.1 us (1%)
    pallas_call x1, Pallas kernels, factor(): pl.pallas_call(factor_kernel, in_specs=[pl.BlockSpec(memory_space=pl.ANY)...  154 us
    all_gather x1, blocking collectives, local(): residual = -lax.all_gather(gradient, 'feat', axis=0, tiled=True)[None, :]  55.2 us
    reduce_scatter x1, waiting for transfers between devices, local(): summed = lax.psum_scatter(mixed, 'ex', scatter_dimension=0, tiled=True)  49.7 us
    ppermute x20, waiting for transfers between devices, butterfly(): lax.ppermute(value, axis, [(s, s ^ mask) for s in range(count)])  39.6 us
    all_gather x1, waiting for transfers between devices, local(): pieces = lax.all_gather(sketch, ('ex', 'feat'), axis=0)  27.6 us
    ppermute x20, starting transfers between devices, butterfly(): lax.ppermute(value, axis, [(s, s ^ mask) for s in range(count)])  27.5 us
    pallas_call x5, Pallas kernels, call(): pl.pallas_call(kernel, in_specs=[VMEM] * len(args), out_specs=[VMEM] * le...  20.4 us
    psum x1, blocking collectives, local(): gradient = lax.psum(grad_part, 'ex') / total_rows + REG / D * weights  13.3 us
  transfers between devices with their start and end apart: 26, of which 24 were waited for; matrix products, arithmetic and copies ran while one was open for 1% of the time, Pallas kernels for 0%

profile of v3, /device:TPU:0, one launch (start us, length us, event | category | flops | bytes accessed | tf_op | source)
XLA Modules:
  0.0 436.8 jit_solution(18426611939354141599)
XLA Ops:
  6.5 3.3 fusion.10
  9.9 3.0 collective-permute-start
  12.9 2.6 collective-permute-start.1
  15.5 0.7 convert_element_type.21
  16.2 1.2 collective-permute-done.1
  17.4 3.5 collective-permute-done.2
  20.9 0.7 convert_subtract_fusion
  21.6 2.0 multiply_convert_fusion
  23.7 1.4 copy-done.1
  25.1 6.6 %fusion = f32[2048,512]{1,0:T(8,128)} fusion(s32[2048]{0:T(1024)S(1)} %iota_add_fusion, s32[2048]{0:T(1024)S(1)} %copy-done.3, bf16[2048,512]{1,0:T(8,128)(2,1)S(1)} %multiply_convert_fusion, bf16[2048]{0:T(1024)(128)(2,1)S(1)} %convert_element_type.21), kind=kOutput, calls=%fused_computation.1 | convolution fusion | flops 4321181696 | bytes 6311936 | tf_op jit(solution)/shard_map/dot_general | solution.py:354
  31.8 0.0 all-gather.4.cloned.1.call-start
  31.8 49.7 %reduce-scatter.2.cloned.1.call-done = f32[256,512]{1,0:T(8,128)} async-done(((f32[2048,512]{1,0:T(8,128)}), f32[256,512]{1,0:T(8,128)}) %reduce-scatter.2.cloned.1.call-update) | async-done | bytes 524304 | tf_op jit(solution)/shard_map/reduce_scatter | solution.py:355
  81.5 1.8 multiply_convert_fusion.1
  83.3 0.0 all-gather.4.cloned.1.call-update
  83.3 4.6 %all-to-all-start = ((bf16[4,512,512]{2,1,0:T(8,128)(2,1)}), bf16[4,512,512]{2,1,0:T(8,128)(2,1)}, u32[]{:S(2)}, u32[]{:S(2)}) async-start(bf16[4,512,512]{2,1,0:T(8,128)(2,1)} %bitcast.25), calls=%async_computation.1 | async-start | bytes 4194304 | tf_op jit(solution)/shard_map/all_to_all | solution.py:362
  87.9 0.9 fusion.11
  88.8 13.3 %psum.7 = f32[512]{0:T(512)S(1)} all-reduce(f32[512]{0:T(512)S(1)} %bitcast.32), channel_id=1, replica_groups=mesh['ex'=8,'feat'=4] {'ex'}, use_global_device_ids=true, to_apply=%region_1.0 | all-reduce | flops 512 | bytes 4096 | tf_op jit(solution)/shard_map/psum | solution.py:361
  102.1 55.2 %all-gather.1 = f32[4,1,512]{2,1,0:T(1,128)S(1)} all-gather(f32[1,1,512]{2,1,0:T(1,128)S(1)} %bitcast.33), channel_id=1, replica_groups=mesh['ex'=8,'feat'=4] {'feat'}, dimensions={0}, use_global_device_ids=true | all-gather | bytes 10240 | tf_op jit(solution)/shard_map/all_gather | solution.py:363
  157.4 2.0 copy.9
  159.4 27.6 %all-gather.4.cloned.1.call-done = bf16[8192,512]{1,0:T(8,128)(2,1)} async-done(((bf16[256,512]{1,0:T(8,128)(2,1)}), bf16[8192,512]{1,0:T(8,128)(2,1)}) %all-gather.4.cloned.1.call-update) | async-done | bytes 8388624 | tf_op jit(solution)/shard_map/all_gather | solution.py:357
  187.0 153.9 %shard_map.64 = (f32[2048,2048]{1,0:T(8,128)S(1)}, f32[2048,128]{1,0:T(8,128)S(1)}) custom-call(bf16[8,4,256,512]{3,2,1,0:T(8,128)(2,1)} %bitcast.24), custom_call_target="tpu_custom_call" | custom-call | tf_op jit(solution)/shard_map/pallas_call | solution.py:179
  340.9 4.5 %shard_map.65 = (f32[1,2048]{1,0:T(1,128)S(1)}, f32[1,1]{1,0:T(1,128)}, f32[1,2048]{1,0:T(1,128)S(1)}) custom-call(f32[2048,2048]{1,0:T(8,128)S(1)} %get-tuple-element.24.lower, f32[2048,128]{1,0:T(8,128)S(1)} %get-tuple-element.25.inverses, bf16[512,2048]{1,0:T(8,128)(2,1)S(1)} %bitcast.18, f32[1,2048]{1,0:T(1,128)S(1)} %bitcast.22), custom_call_target="tpu_custom_call" | custom-call | tf_op jit(solution)/shard_map/pallas_call | solution.py:308
  345.4 0.3 collective-permute-start.3
  345.7 0.9 collective-permute-done.3
  346.6 1.5 collective-permute-start.4
  348.1 2.2 collective-permute-done.4
  350.4 1.6 collective-permute-start.5
  351.9 2.2 collective-permute-done.5
  354.1 1.6 collective-permute-start.6
  355.7 2.1 collective-permute-done.6
  357.8 2.0 collective-permute-start.7
  359.8 2.6 collective-permute-done.7
  362.5 5.0 %shard_map.66 = (f32[1,2048]{1,0:T(1,128)S(1)}, f32[1,2048]{1,0:T(1,128)S(1)}, f32[1,2048]{1,0:T(1,128)S(1)}, f32[1,1]{1,0:T(1,128)}, f32[1,2048]{1,0:T(1,128)S(1)}) custom-call(f32[2048,2048]{1,0:T(8,128)S(1)} %get-tuple-element.24.lower, f32[2048,128]{1,0:T(8,128)S(1)} %get-tuple-element.25.inverses, bf16[512,2048]{1,0:T(8,128)(2,1)S(1)} %bitcast.19, ...), custom_call_target="tpu_custom_call" | custom-call | tf_op jit(solution)/shard_map/pallas_call | solution.py:308
  367.4 1.2 collective-permute-done.8
  368.6 1.5 collective-permute-start.9
  370.1 2.2 collective-permute-done.9
  372.3 1.6 collective-permute-start.10
  373.9 2.2 collective-permute-done.10
  376.1 1.7 collective-permute-start.11
  377.7 2.1 collective-permute-done.11
  379.8 2.1 collective-permute-start.12
  381.9 2.5 collective-permute-done.12
  384.4 4.9 %shard_map.67 = (f32[1,2048]{1,0:T(1,128)S(1)}, f32[1,2048]{1,0:T(1,128)S(1)}, f32[1,2048]{1,0:T(1,128)S(1)}, f32[1,1]{1,0:T(1,128)}, f32[1,2048]{1,0:T(1,128)S(1)}) custom-call(f32[2048,2048]{1,0:T(8,128)S(1)} %get-tuple-element.24.lower, f32[2048,128]{1,0:T(8,128)S(1)} %get-tuple-element.25.inverses, bf16[512,2048]{1,0:T(8,128)(2,1)S(1)} %bitcast.20, ...), custom_call_target="tpu_custom_call" | custom-call | tf_op jit(solution)/shard_map/pallas_call | solution.py:308
  389.3 1.2 collective-permute-done.13
  390.5 1.5 collective-permute-start.14
  392.0 2.2 collective-permute-done.14
  394.2 1.6 collective-permute-start.15
  395.8 2.2 collective-permute-done.15
  398.0 1.7 collective-permute-start.16
  399.6 2.1 collective-permute-done.16
  401.7 2.1 collective-permute-start.17
  403.8 2.5 collective-permute-done.17
  406.3 5.1 %shard_map.68 = (f32[1,2048]{1,0:T(1,128)S(1)}, f32[1,2048]{1,0:T(1,128)}, f32[1,2048]{1,0:T(1,128)S(1)}, f32[1,1]{1,0:T(1,128)}, f32[1,2048]{1,0:T(1,128)S(1)}) custom-call(f32[2048,2048]{1,0:T(8,128)S(1)} %get-tuple-element.24.lower, f32[2048,128]{1,0:T(8,128)S(1)} %get-tuple-element.25.inverses, bf16[512,2048]{1,0:T(8,128)(2,1)S(1)} %bitcast.21, ...), custom_call_target="tpu_custom_call" | custom-call | tf_op jit(solution)/shard_map/pallas_call | solution.py:308
  411.4 1.2 collective-permute-done.18
  412.6 1.5 collective-permute-start.19
  414.0 2.2 collective-permute-done.19
  416.3 1.6 collective-permute-start.20
  417.8 2.2 collective-permute-done.20
  420.0 1.7 collective-permute-start.21
  421.7 2.0 collective-permute-done.21
  423.8 2.1 collective-permute-start.22
  426.6 1.8 collective-permute-done.22
  428.4 1.0 shard_map.69
  429.4 0.6 add.123
  (41 shorter events, 0.3 us)
Async XLA Ops:
  6.5 18.5 %copy-start.3 = (s32[2048]{0:T(1024)S(1)}, s32[2048]{0:T(1024)}, u32[]{:S(2)}) copy-start(s32[2048]{0:T(1024)} %param.10) | copy-start | bytes 24580
  6.5 74.9 %reduce-scatter.2.cloned.1.call-start = ((), (), s32[]{:S(2)}) async-start(), calls=%async_computation.2 | async-start | bytes 4718592 | tf_op jit(solution)/shard_map/reduce_scatter | solution.py:355
  9.9 6.3 %collective-permute-start = (f32[2048]{0:T(1024)S(1)}, f32[2048]{0:T(1024)S(1)}, u32[]{:S(2)}, u32[]{:S(2)}) collective-permute-start(f32[2048]{0:T(1024)S(1)} %bitcast.27), channel_id=1, source_target_pairs={{0,1},{1,0},{2,3},{3,2},{4,5},{5,4},{6,7},{7,6},{8,9},{9,8},{10,11... | collective-permute-start | bytes 24584 | tf_op jit(solution)/shard_map/ppermute | solution.py:322
  12.9 4.5 %collective-permute-start.1 = (f32[2048]{0:T(1024)S(1)}, f32[2048]{0:T(1024)S(1)}, u32[]{:S(2)}, u32[]{:S(2)}) collective-permute-start(f32[2048]{0:T(1024)S(1)} %bitcast.28), channel_id=1, source_target_pairs={{0,2},{1,3},{2,0},{3,1},{4,6},{5,7},{6,4},{7,5},{8,10},{9,11},{10,... | collective-permute-start | bytes 24584 | tf_op jit(solution)/shard_map/ppermute | solution.py:322
  15.5 5.4 %collective-permute-start.2 = (f32[2048]{0:T(1024)S(1)}, f32[2048]{0:T(1024)S(1)}, u32[]{:S(2)}, u32[]{:S(2)}) collective-permute-start(f32[2048]{0:T(1024)S(1)} %bitcast.29), channel_id=1, source_target_pairs={{0,3},{1,2},{2,1},{3,0},{4,7},{5,6},{6,5},{7,4},{8,11},{9,10},{10,... | collective-permute-start | bytes 24584 | tf_op jit(solution)/shard_map/ppermute | solution.py:322
  23.7 1.4 copy-start.1
  31.7 56.2 %copy-start = (bf16[2048,512]{1,0:T(8,128)(2,1)S(1)}, bf16[2048,512]{1,0:T(8,128)(2,1)}, u32[]{:S(2)}) copy-start(bf16[2048,512]{1,0:T(8,128)(2,1)} %param.6) | copy-start | bytes 6291460
  31.7 70.4 %copy-start.2 = (f32[512]{0:T(512)S(1)}, f32[512]{0:T(512)}, u32[]{:S(2)}) copy-start(f32[512]{0:T(512)} %param.7) | copy-start | bytes 6148
  31.8 155.2 %all-gather.4.cloned.1.call-start = ((), (), s32[]{:S(2)}) async-start(), calls=%async_computation.3 | async-start | bytes 8650752 | tf_op jit(solution)/shard_map/all_gather | solution.py:357
  83.3 74.1 %all-to-all-start = ((bf16[4,512,512]{2,1,0:T(8,128)(2,1)}), bf16[4,512,512]{2,1,0:T(8,128)(2,1)}, u32[]{:S(2)}, u32[]{:S(2)}) async-start(bf16[4,512,512]{2,1,0:T(8,128)(2,1)} %bitcast.25), calls=%async_computation.1 | async-start | bytes 4194304 | tf_op jit(solution)/shard_map/all_to_all | solution.py:362
  345.4 1.2 collective-permute-start.3
  346.6 3.7 collective-permute-start.4
  350.4 3.7 collective-permute-start.5
  354.1 3.7 collective-permute-start.6
  357.8 4.6 %collective-permute-start.7 = (f32[1,2048]{1,0:T(1,128)S(1)}, f32[1,2048]{1,0:T(1,128)S(1)}, u32[]{:S(2)}, u32[]{:S(2)}) collective-permute-start(f32[1,2048]{1,0:T(1,128)S(1)} %add.105), channel_id=1, source_target_pairs={{0,2},{1,3},{2,0},{3,1},{4,6},{5,7},{6,4},{7,5},{8,10},{9,11},{10,... | collective-permute-start | bytes 24584 | tf_op jit(solution)/shard_map/ppermute | solution.py:331
  367.4 1.2 collective-permute-start.8
  368.6 3.7 collective-permute-start.9
  372.3 3.7 collective-permute-start.10
  376.1 3.7 collective-permute-start.11
  379.8 4.6 %collective-permute-start.12 = (f32[1,2048]{1,0:T(1,128)S(1)}, f32[1,2048]{1,0:T(1,128)S(1)}, u32[]{:S(2)}, u32[]{:S(2)}) collective-permute-start(f32[1,2048]{1,0:T(1,128)S(1)} %add.110), channel_id=1, source_target_pairs={{0,2},{1,3},{2,0},{3,1},{4,6},{5,7},{6,4},{7,5},{8,10},{9,11},{10,... | collective-permute-start | bytes 24584 | tf_op jit(solution)/shard_map/ppermute | solution.py:331
  389.3 1.2 collective-permute-start.13
  390.5 3.7 collective-permute-start.14
  394.2 3.7 collective-permute-start.15
  398.0 3.7 collective-permute-start.16
  401.7 4.6 %collective-permute-start.17 = (f32[1,2048]{1,0:T(1,128)S(1)}, f32[1,2048]{1,0:T(1,128)S(1)}, u32[]{:S(2)}, u32[]{:S(2)}) collective-permute-start(f32[1,2048]{1,0:T(1,128)S(1)} %add.115), channel_id=1, source_target_pairs={{0,2},{1,3},{2,0},{3,1},{4,6},{5,7},{6,4},{7,5},{8,10},{9,11},{10,... | collective-permute-start | bytes 24584 | tf_op jit(solution)/shard_map/ppermute | solution.py:331
  411.4 1.2 collective-permute-start.18
  412.6 3.7 collective-permute-start.19
  416.3 3.7 collective-permute-start.20
  420.0 3.7 collective-permute-start.21
  423.8 4.6 %collective-permute-start.22 = (f32[1,2048]{1,0:T(1,128)S(1)}, f32[1,2048]{1,0:T(1,128)S(1)}, u32[]{:S(2)}, u32[]{:S(2)}) collective-permute-start(f32[1,2048]{1,0:T(1,128)S(1)} %add.120), channel_id=1, source_target_pairs={{0,2},{1,3},{2,0},{3,1},{4,6},{5,7},{6,4},{7,5},{8,10},{9,11},{10,... | collective-permute-start | bytes 24584 | tf_op jit(solution)/shard_map/ppermute | solution.py:331
Sparse Core Ops, SparseCore 0:
  31.9 49.5 reduce-scatter.1
  84.8 102.1 all-gather.3
